TPU v7x, 32 devices: a whole 2x2x4 slice. The times are simulated.
32 devices in a mesh: lat: 8 (over z, y), lon: 4 (over x, core).
Axes of the slice: x: 2, y: 2, z: 4, core: 2. Of those that a mesh axis runs over, the one named last changes fastest.
Arguments:
- state: bfloat16 [48, 1440, 512], P('lat', 'lon'), may hold values from -6 to 6
- filter_values: float32 [3, 48, 3, 8], replicated, may hold values from -2 to 2
- offsets: int32 [48, 3, 8], replicated, may hold values from -720 to 719, as said below
- mixing: bfloat16 [3, 512, 512], replicated, may hold values from -0.15625 to 0.15625
- cotangent: bfloat16 [48, 1440, 512], P('lat', 'lon'), may hold values from -6 to 6
Outputs:
- output: bfloat16 [48, 1440, 512], P('lat', 'lon')
- mixing_grad: float32 [3, 512, 512], P(None, 'lat', 'lon')
- state_grad: bfloat16 [48, 1440, 512], P('lat', 'lon')
Inputs may be any that keep to these rules, and one draw needn't show every extreme that they name: On cycles i with i < 1 or i >= 47 an offset may reach half the cycle; on all other cycles -16 <= offsets[i, d, s] <= 16, and both 16 and -16 occur there.
All inputs are finite; a program needn't handle non-finite values.
Results may differ from a plain program's by a relative error of at most 0.0055.
Values may be sent and summed in bfloat16 or wider, within the bound.
A program may use at most 192 MiB of HBM per device.

v0:
```python
import math

import jax
import jax.numpy as jnp
import numpy as np
from jax import lax
from jax.sharding import PartitionSpec as P

HALO = 16
POLAR = 1


def with_halo(shard, sides, width, wrap):
    for axis, dim in sides:
        count, length = (lax.axis_size(axis), shard.shape[dim])
        up = [(i, (i + 1) % count) for i in range(count if wrap else count - 1)]
        down = [(j, i) for i, j in up]
        last = lax.slice_in_dim(shard, length - width, length, axis=dim)
        leading = lax.slice_in_dim(shard, 0, width, axis=dim)
        before = lax.ppermute(last, axis, up)
        after = lax.ppermute(leading, axis, down)
        shard = jnp.concatenate([before, shard, after], axis=dim)
    return shard


def gelu_value(value):
    return 0.5 * value * (1.0 + jax.scipy.special.erf(value * 0.7071067811865476))


def gelu_slope(value):
    rising = 0.5 * (1.0 + jax.scipy.special.erf(value * 0.7071067811865476))
    return rising + value * jnp.exp(-0.5 * value * value) * 0.3989422804014327


def near_terms(source, psi_loc, off_loc, polar_pad, adjoint, rows, width):
    targets = np.arange(rows)
    span = source.shape[1]
    columns = jnp.arange(width, dtype=jnp.int32)
    places = jnp.arange(span, dtype=jnp.int32)
    widened = source.astype(jnp.float32)
    summed = None
    for d in range(3):
        if adjoint:
            first = 2 - d
            weight_rows = targets + 2 - d
        else:
            first = d
            weight_rows = targets + 1
        keep = 1.0 - polar_pad[weight_rows]
        weights = psi_loc[:, weight_rows, d, :] * keep[None, :, None]
        shifts = off_loc[weight_rows, d, :]
        if adjoint:
            shifts = -shifts
        shifts = jnp.clip(shifts, -HALO, HALO)
        col_index = HALO + columns[None, None, :] + shifts[:, :, None]
        onehot = (col_index[..., None] == places[None, None, None, :]).astype(jnp.float32)
        band = jnp.einsum("krs,rsjm->krjm", weights, onehot, precision=lax.Precision.HIGHEST)
        source_rows = widened[first : first + rows]
        term = jnp.einsum("krjm,rmc->krjc", band, source_rows, precision=lax.Precision.HIGHEST)
        summed = term if summed is None else summed + term
    return summed


def convolve(field, psi_loc, off_loc, polar_pad, adjoint):
    rows, width = (field.shape[0], field.shape[1])
    cycle_len = width * lax.axis_size("lon")
    lon_start = lax.axis_index("lon") * width
    columns = jnp.arange(width, dtype=jnp.int32)
    padded = with_halo(field, (("lat", 0),), 1, False)
    wide = with_halo(padded, (("lon", 1),), HALO, True)
    summed = near_terms(wide, psi_loc, off_loc, polar_pad, adjoint, rows, width)
    if adjoint:
        picks = np.array([0, rows - 1])
        items = [(0, 0, 1, 1), (1, 0, 1, 2), (rows - 2, 1, rows, 0), (rows - 1, 1, rows, 1)]
        sign = -1
    else:
        picks = np.array([0, 1, rows - 2, rows - 1])
        items = [(0, 0, 1, 1), (0, 1, 1, 2), (rows - 1, 2, rows, 0), (rows - 1, 3, rows, 1)]
        sign = 1
    cycles = lax.all_gather(field[picks], "lon", axis=1, tiled=True)
    for target, cycle_pos, weight_row, d in items:
        weights = psi_loc[:, weight_row, d, :] * polar_pad[weight_row]
        col_index = (
            lon_start + columns[None, :] + sign * off_loc[weight_row, d, :][:, None]
        ) % cycle_len
        picked = cycles[cycle_pos][col_index].astype(jnp.float32)
        contrib = jnp.einsum("ks,sjc->kjc", weights, picked, precision=lax.Precision.HIGHEST)
        summed = summed.at[:, target].add(contrib)
    return summed.astype(jnp.bfloat16)


def per_device(state, filter_values, offsets, mixing, cotangent):
    rows, width, chans = state.shape
    nrings = offsets.shape[0]
    cycle_len = width * lax.axis_size("lon")
    lat_start = lax.axis_index("lat") * rows
    psi_pad = jnp.pad(filter_values, ((0, 0), (1, 1), (0, 0), (0, 0)))
    off_pad = jnp.pad(offsets, ((1, 1), (0, 0), (0, 0)))
    psi_loc = lax.dynamic_slice_in_dim(psi_pad, lat_start, rows + 2, 1)
    off_loc = lax.dynamic_slice_in_dim(off_pad, lat_start, rows + 2, 0)
    global_rows = lat_start + jnp.arange(rows + 2, dtype=jnp.int32) - 1
    polar_pad = ((global_rows < POLAR) | (global_rows >= nrings - POLAR)).astype(jnp.float32)
    filtered = convolve(state, psi_loc, off_loc, polar_pad, False)
    mixed = jnp.einsum("krjc,kcd->rjd", filtered, mixing, preferred_element_type=jnp.float32)
    output = (state.astype(jnp.float32) + gelu_value(mixed)).astype(jnp.bfloat16)
    slope = (cotangent.astype(jnp.float32) * gelu_slope(mixed)).astype(jnp.bfloat16)
    norm_scale = 1.0 / math.sqrt(nrings * cycle_len)
    local_grad = (
        jnp.einsum("krjc,rjd->kcd", filtered, slope, preferred_element_type=jnp.float32)
        * norm_scale
    )
    partial_grad = lax.psum_scatter(local_grad, "lat", scatter_dimension=1, tiled=True)
    mixing_grad = lax.psum_scatter(partial_grad, "lon", scatter_dimension=2, tiled=True)
    spread = convolve(slope, psi_loc, off_loc, polar_pad, True)
    back = jnp.einsum("krjd,kcd->rjc", spread, mixing, preferred_element_type=jnp.float32)
    state_grad = (cotangent.astype(jnp.float32) + back).astype(jnp.bfloat16)
    return (output, mixing_grad, state_grad)


def solution(mesh):
    in_specs = (P("lat", "lon", None), P(), P(), P(), P("lat", "lon", None))
    out_specs = (P("lat", "lon", None), P(None, "lat", "lon"), P("lat", "lon", None))
    return jax.shard_map(
        per_device, mesh=mesh, in_specs=in_specs, out_specs=out_specs, check_vma=False
    )
```

profile of v0, /device:TPU:0, one launch (start us, length us, event | category | flops | bytes accessed | tf_op | source)
XLA Modules:
  0.0 551.8 jit_solution(17384894505720918365)
XLA Ops:
  28.0 14.2 %fusion.35 = f32[3,6,360,392]{2,0,3,1:T(4,128)} fusion(s32[6,8,360]{2,1,0:T(8,128)S(1)} %get-tuple-element.140, f32[6,3,8]{2,1,0:T(4,128)S(1)} %gather_fusion.4, f32[6]{0:T(128)S(1)} %broadcast_subtract_fusion.2), kind=kOutput, calls=%fused_computation.60 | convolution fusion | flops 250629264 | bytes 10230360 | tf_op jit(solution)/shard_map/krs,rsjm->krjm/dot_general | solution.py:57
  46.9 15.1 %fusion.34 = f32[3,6,360,392]{2,0,3,1:T(4,128)} fusion(s32[6,8,360]{2,1,0:T(8,128)} %get-tuple-element.141, f32[6,3,8]{2,1,0:T(4,128)S(1)} %gather_fusion.6, f32[6]{0:T(128)S(1)} %broadcast_subtract_fusion.2), kind=kOutput, calls=%fused_computation.59 | convolution fusion | flops 250629264 | bytes 10230360 | tf_op jit(solution)/shard_map/krs,rsjm->krjm/dot_general | solution.py:57
  62.0 7.4 %iota_compare_fusion.5 = pred[6,8,360,392]{2,3,1,0:T(8,128)(4,1)} fusion(s32[6,8,360]{2,1,0:T(8,128)S(1)} %copy-done.14), kind=kLoop, calls=%fused_computation.28 | loop fusion | flops 6773760 | bytes 6842880 | tf_op jit(solution)/shard_map/eq | solution.py:56
  69.5 16.7 %fusion.28 = f32[3,6,360,392]{2,0,3,1:T(4,128)} fusion(pred[6,8,360,392]{2,3,1,0:T(8,128)(4,1)} %iota_compare_fusion.5, f32[6,3,8]{2,1,0:T(4,128)S(1)} %copy-done.34, f32[6]{0:T(128)S(1)} %broadcast_subtract_fusion.2), kind=kOutput, calls=%fused_computation.55 | convolution fusion | flops 243855504 | bytes 16935000 | tf_op jit(solution)/shard_map/krs,rsjm->krjm/dot_general | solution.py:57
  100.0 18.4 %fusion.22 = f32[6,512,3,360]{1,3,2,0:T(8,128)} fusion(f32[3,6,360,392]{2,0,3,1:T(4,128)} %fusion.28, bf16[8,392,512]{2,1,0:T(8,128)(2,1)S(1)} %pad_maximum_fusion), kind=kOutput, calls=%fused_computation.53 | convolution fusion | flops 15606743040 | bytes 25840128 | tf_op jit(solution)/shard_map/krjm,rmc->krjc/dot_general | solution.py:59
  118.4 18.4 %fusion.20 = f32[6,512,3,360]{1,3,2,0:T(8,128)} fusion(f32[3,6,360,392]{2,0,3,1:T(4,128)} %fusion.35, bf16[8,392,512]{2,1,0:T(8,128)(2,1)S(1)} %pad_maximum_fusion), kind=kOutput, calls=%fused_computation.51 | convolution fusion | flops 15606743040 | bytes 25840128 | tf_op jit(solution)/shard_map/krjm,rmc->krjc/dot_general | solution.py:59
  136.8 31.0 %add_bitcast_fusion.1 = f32[3,6,360,512]{3,2,0,1:T(8,128)} fusion(f32[6,512,3,360]{1,3,2,0:T(8,128)} %fusion.22, f32[6,512,3,360]{1,3,2,0:T(8,128)} %fusion.20, f32[3,6,360,392]{2,0,3,1:T(4,128)} %fusion.34, bf16[8,392,512]{2,1,0:T(8,128)(2,1)S(1)} %pad_maximum_fusion), kind=kOutput, calls=%fused_computation.42 | convolution fusion | flops 15613378560 | bytes 52382208 | tf_op jit(solution)/shard_map/krjm,rmc->krjc/dot_general | solution.py:59
  167.9 11.7 %copy.166 = f32[3,6,360,512]{3,2,0,1:T(8,128)} copy(f32[3,6,360,512]{3,2,0,1:T(8,128)} %add_bitcast_fusion.1) | data formatting | bytes 26542080
  184.5 11.4 %gather_fusion.8 = bf16[2880,512]{1,0:T(8,128)(2,1)} fusion(bf16[1440,512]{1,0:T(8,128)(2,1)} %get-tuple-element.110, s32[3072]{0:T(1024)S(1)} %copy-done.30), kind=kCustom, calls=%fused_computation.8 | custom fusion | bytes 5909760 | tf_op jit(solution)/shard_map/gather | solution.py:86
  195.9 6.9 %fusion.67 = f32[3,360,512]{2,0,1:T(4,128)} fusion(bf16[8,360,512]{2,1,0:T(8,128)(2,1)} %bitcast.232, s32[]{:T(128)S(6)} %add.727, s32[]{:T(128)S(6)} %add.728, f32[3,48,3,8]{3,0,2,1:T(4,128)S(1)} %copy.74, f32[]{:T(128)} %bitcast.19), kind=kOutput, calls=%fused_computation.100 | convolution fusion | flops 53084184 | bytes 5174796 | tf_op jit(solution)/shard_map/ks,sjc->kjc/dot_general | solution.py:87
  202.8 11.2 %gather_fusion.9 = bf16[2880,512]{1,0:T(8,128)(2,1)} fusion(bf16[1440,512]{1,0:T(8,128)(2,1)} %get-tuple-element.109, s32[3072]{0:T(1024)S(1)} %copy-done.29), kind=kCustom, calls=%fused_computation.9 | custom fusion | bytes 5909760 | tf_op jit(solution)/shard_map/gather | solution.py:86
  227.9 11.6 %copy.168 = f32[3,6,360,512]{3,2,0,1:T(8,128)} copy(f32[3,6,360,512]{3,2,0,1:T(8,128)} %fusion.75) | data formatting | bytes 26542080
  239.5 11.6 %gather_fusion.10 = bf16[2880,512]{1,0:T(8,128)(2,1)} fusion(bf16[1440,512]{1,0:T(8,128)(2,1)} %get-tuple-element.108, s32[3072]{0:T(1024)S(1)} %copy-done.28), kind=kCustom, calls=%fused_computation.10 | custom fusion | bytes 5909760 | tf_op jit(solution)/shard_map/gather | solution.py:86
  251.2 6.8 %fusion.63 = f32[3,360,512]{2,0,1:T(4,128)} fusion(bf16[8,360,512]{2,1,0:T(8,128)(2,1)} %bitcast.228, s32[]{:T(128)S(6)} %add.735, f32[3,48,3,8]{3,0,2,1:T(4,128)S(1)} %copy.74, f32[]{:T(128)} %bitcast.32), kind=kOutput, calls=%fused_computation.96 | convolution fusion | flops 53084184 | bytes 5174792 | tf_op jit(solution)/shard_map/ks,sjc->kjc/dot_general | solution.py:87
  258.0 9.5 %gather_fusion.11 = bf16[2880,512]{1,0:T(8,128)(2,1)} fusion(bf16[1440,512]{1,0:T(8,128)(2,1)S(1)} %get-tuple-element.107, s32[3072]{0:T(1024)S(1)} %copy-done.31), kind=kCustom, calls=%fused_computation.11 | custom fusion | bytes 5909760 | tf_op jit(solution)/shard_map/gather | solution.py:86
  267.5 5.5 fusion.61
  281.7 10.2 %fusion.38 = (bf16[6,360,512]{2,1,0:T(8,128)(2,1)}, bf16[6,360,512]{2,1,0:T(8,128)(2,1)}) fusion(bf16[6,360,512]{2,1,0:T(8,128)(2,1)S(1)} %copy-done.37, bf16[6,360,512]{2,1,0:T(8,128)(2,1)S(1)} %copy-done.7, bf16[3,512,512]{2,1,0:T(8,128)(2,1)S(1)} %copy-done, f32[3,6,360,512]{3,2,0,1:T(8,128)} %fusion.74), kind=kOutput, calls=%fused_computation.66 | convolution fusion | flops 3418398720 | bytes 23691264 | tf_op jit(solution)/shard_map/krjc,kcd->rjd/dot_general | solution.py:104
  296.5 14.4 %fusion.32 = f32[3,6,360,392]{2,0,3,1:T(4,128)} fusion(s32[6,8,360]{2,1,0:T(8,128)S(1)} %copy-done.13, f32[6,3,8]{2,1,0:T(4,128)S(1)} %copy-done.23, f32[6]{0:T(128)S(1)} %broadcast_subtract_fusion.2), kind=kOutput, calls=%fused_computation.57 | convolution fusion | flops 250629264 | bytes 10230360 | tf_op jit(solution)/shard_map/krs,rsjm->krjm/dot_general | solution.py:57
  310.9 14.1 %fusion.33 = f32[3,6,360,392]{2,0,3,1:T(4,128)} fusion(s32[6,8,360]{2,1,0:T(8,128)S(1)} %copy-done.12, f32[6,3,8]{2,1,0:T(4,128)S(1)} %gather_fusion.13, f32[6]{0:T(128)S(1)} %copy-done.33), kind=kOutput, calls=%fused_computation.58 | convolution fusion | flops 250629264 | bytes 10230360 | tf_op jit(solution)/shard_map/krs,rsjm->krjm/dot_general | solution.py:57
  325.0 14.4 %fusion.31 = f32[3,6,360,392]{2,0,3,1:T(4,128)} fusion(s32[6,8,360]{2,1,0:T(8,128)S(1)} %copy-done.11, f32[6,3,8]{2,1,0:T(4,128)S(1)} %gather_fusion.16, f32[6]{0:T(128)S(1)} %broadcast_subtract_fusion.1), kind=kOutput, calls=%fused_computation.56 | convolution fusion | flops 250629264 | bytes 10230360 | tf_op jit(solution)/shard_map/krs,rsjm->krjm/dot_general | solution.py:57
  347.4 6.9 %collective-permute-done.5 = bf16[1,360,512]{2,1,0:T(8,128)(2,1)S(1)} collective-permute-done((bf16[1,360,512]{2,1,0:T(8,128)(2,1)S(1)}, bf16[1,360,512]{2,1,0:T(8,128)(2,1)S(1)}, u32[]{:S(2)}, u32[]{:S(2)}) %collective-permute-start.5) | collective-permute-done | bytes 368672 | tf_op jit(solution)/shard_map/ppermute | solution.py:21
  354.3 8.1 %collective-permute-done.4 = bf16[1,360,512]{2,1,0:T(8,128)(2,1)S(1)} collective-permute-done((bf16[1,360,512]{2,1,0:T(8,128)(2,1)S(1)}, bf16[1,360,512]{2,1,0:T(8,128)(2,1)S(1)}, u32[]{:S(2)}, u32[]{:S(2)}) %collective-permute-start.4) | collective-permute-done | bytes 368672 | tf_op jit(solution)/shard_map/ppermute | solution.py:20
  364.0 10.7 %bitcast_multiply_fusion.2 = f32[3,512,512]{2,1,0:T(8,128)} fusion(bf16[6,360,512]{2,1,0:T(8,128)(2,1)S(1)} %copy-done.3, f32[3,6,360,512]{3,2,0,1:T(8,128)} %fusion.74), kind=kOutput, calls=%fused_computation.85 | convolution fusion | flops 3401490432 | bytes 18628608 | tf_op jit(solution)/shard_map/krjc,rjd->kcd/dot_general | solution.py:109
  377.8 18.4 %fusion.16 = f32[6,512,3,360]{1,3,2,0:T(8,128)} fusion(f32[3,6,360,392]{2,0,3,1:T(4,128)} %fusion.33, bf16[8,392,512]{2,1,0:T(8,128)(2,1)S(1)} %pad_maximum_fusion.1), kind=kOutput, calls=%fused_computation.47 | convolution fusion | flops 15606743040 | bytes 25840128 | tf_op jit(solution)/shard_map/krjm,rmc->krjc/dot_general | solution.py:59
  396.2 19.1 %fusion.14 = f32[6,512,3,360]{1,3,2,0:T(8,128)} fusion(f32[3,6,360,392]{2,0,3,1:T(4,128)} %fusion.32, bf16[8,392,512]{2,1,0:T(8,128)(2,1)S(1)} %pad_maximum_fusion.1), kind=kOutput, calls=%fused_computation.45 | convolution fusion | flops 15606743040 | bytes 25840128 | tf_op jit(solution)/shard_map/krjm,rmc->krjc/dot_general | solution.py:59
  415.3 31.0 %add_bitcast_fusion = f32[3,6,360,512]{3,2,0,1:T(8,128)} fusion(f32[6,512,3,360]{1,3,2,0:T(8,128)} %fusion.16, f32[6,512,3,360]{1,3,2,0:T(8,128)} %fusion.14, f32[3,6,360,392]{2,0,3,1:T(4,128)} %fusion.31, bf16[8,392,512]{2,1,0:T(8,128)(2,1)S(1)} %pad_maximum_fusion.1), kind=kOutput, calls=%fused_computation.41 | convolution fusion | flops 15613378560 | bytes 52382208 | tf_op jit(solution)/shard_map/krjm,rmc->krjc/dot_general | solution.py:59
  449.4 11.3 %gather_fusion.19 = bf16[2880,512]{1,0:T(8,128)(2,1)} fusion(bf16[1440,512]{1,0:T(8,128)(2,1)} %get-tuple-element.114, s32[3072]{0:T(1024)S(1)} %pad_clamp_fusion.3), kind=kCustom, calls=%fused_computation.19 | custom fusion | bytes 5909760 | tf_op jit(solution)/shard_map/gather | solution.py:86
  460.7 11.2 %gather_fusion.20 = bf16[2880,512]{1,0:T(8,128)(2,1)} fusion(bf16[1440,512]{1,0:T(8,128)(2,1)} %get-tuple-element.114, s32[3072]{0:T(1024)S(1)} %pad_clamp_fusion.2), kind=kCustom, calls=%fused_computation.20 | custom fusion | bytes 5909760 | tf_op jit(solution)/shard_map/gather | solution.py:86
  471.9 9.5 %gather_fusion.21 = bf16[2880,512]{1,0:T(8,128)(2,1)} fusion(bf16[1440,512]{1,0:T(8,128)(2,1)S(1)} %get-tuple-element.113, s32[3072]{0:T(1024)S(1)} %pad_clamp_fusion.1), kind=kCustom, calls=%fused_computation.21 | custom fusion | bytes 5909760 | tf_op jit(solution)/shard_map/gather | solution.py:86
  481.5 9.7 %gather_fusion.22 = bf16[2880,512]{1,0:T(8,128)(2,1)} fusion(bf16[1440,512]{1,0:T(8,128)(2,1)S(1)} %get-tuple-element.113, s32[3072]{0:T(1024)S(1)} %pad_clamp_fusion), kind=kCustom, calls=%fused_computation.22 | custom fusion | bytes 5909760 | tf_op jit(solution)/shard_map/gather | solution.py:86
  522.7 10.1 %fusion.39 = bf16[6,360,512]{2,1,0:T(8,128)(2,1)} fusion(bf16[6,360,512]{2,1,0:T(8,128)(2,1)} %param.53, f32[3,6,360,512]{3,2,0,1:T(8,128)} %fusion.69, bf16[3,512,512]{2,1,0:T(8,128)(2,1)S(1)} %copy-done), kind=kOutput, calls=%fused_computation.67 | convolution fusion | flops 3404021760 | bytes 19267584 | tf_op jit(solution)/shard_map/krjd,kcd->rjc/dot_general | solution.py:115
  532.8 12.0 %reduce-scatter.5.cloned.1.call-done = f32[3,64,128]{2,1,0:T(8,128)} async-done(((f32[3,64,512]{2,1,0:T(8,128)}), f32[3,64,128]{2,1,0:T(8,128)}) %reduce-scatter.5.cloned.1.call-update) | async-done | bytes 98320 | tf_op jit(solution)/shard_map/reduce_scatter | solution.py:113
  (178 shorter events, 118.3 us)
Async XLA Ops:
  7.2 274.4 %copy-start = (bf16[3,512,512]{2,1,0:T(8,128)(2,1)S(1)}, bf16[3,512,512]{2,1,0:T(8,128)(2,1)}, u32[]{:S(2)}) copy-start(bf16[3,512,512]{2,1,0:T(8,128)(2,1)} %param.52) | copy-start | bytes 4718596
  7.2 14.2 %copy-start.16 = (s32[6]{0:T(128)S(1)}, s32[6]{0:T(128)}, u32[]{:S(2)}) copy-start(s32[6]{0:T(128)} %constant.472) | copy-start | bytes 76
  7.2 14.8 %copy-start.21 = (s32[6]{0:T(128)S(1)}, s32[6]{0:T(128)}, u32[]{:S(2)}) copy-start(s32[6]{0:T(128)} %constant.489) | copy-start | bytes 76
  7.2 15.4 %copy-start.19 = (s32[6]{0:T(128)S(1)}, s32[6]{0:T(128)}, u32[]{:S(2)}) copy-start(s32[6]{0:T(128)} %constant.539) | copy-start | bytes 76
  7.2 15.9 %copy-start.20 = (s32[6]{0:T(128)S(1)}, s32[6]{0:T(128)}, u32[]{:S(2)}) copy-start(s32[6]{0:T(128)} %constant.505) | copy-start | bytes 76
  7.3 17.1 %copy-start.32 = (f32[3,48,3,8]{1,3,2,0:T(8,128)S(1)}, f32[3,48,3,8]{1,3,2,0:T(8,128)}, u32[]{:S(2)}) copy-start(f32[3,48,3,8]{1,3,2,0:T(8,128)} %param.50) | copy-start | bytes 41476
  7.3 172.3 %all-gather.5.cloned.1.call-start = ((), (), s32[]{:S(2)}) async-start(), calls=%async_computation.4 | async-start | bytes 7372800 | tf_op jit(solution)/shard_map/all_gather | solution.py:80
  8.6 79.5 %collective-permute-start = (bf16[1,360,512]{2,1,0:T(8,128)(2,1)S(1)}, bf16[1,360,512]{2,1,0:T(8,128)(2,1)S(1)}, u32[]{:S(2)}, u32[]{:S(2)}) collective-permute-start(bf16[1,360,512]{2,1,0:T(8,128)(2,1)S(1)} %get-tuple-element.122), channel_id=1, source_target_pairs={{0,4},{4,8},{8,12},{12,16},{16,20},{20,24},{24,28},{1,5},{5,9},{9,... | collective-permute-start | bytes 1105928 | tf_op jit(solution)/shard_map/ppermute | solution.py:20
  13.5 76.4 %collective-permute-start.1 = (bf16[1,360,512]{2,1,0:T(8,128)(2,1)S(1)}, bf16[1,360,512]{2,1,0:T(8,128)(2,1)S(1)}, u32[]{:S(2)}, u32[]{:S(2)}) collective-permute-start(bf16[1,360,512]{2,1,0:T(8,128)(2,1)S(1)} %get-tuple-element.121), channel_id=1, source_target_pairs={{4,0},{8,4},{12,8},{16,12},{20,16},{24,20},{28,24},{5,1},{9,5},{13... | collective-permute-start | bytes 1105928 | tf_op jit(solution)/shard_map/ppermute | solution.py:21
  19.4 426.9 %all-gather.7.cloned.1.call-start = ((), (), s32[]{:S(2)}) async-start(), calls=%async_computation.5 | async-start | bytes 3686400 | tf_op jit(solution)/shard_map/all_gather | solution.py:80
  25.8 16.4 %copy-start.22 = (f32[6,3,8]{2,1,0:T(4,128)}, f32[6,3,8]{2,1,0:T(4,128)S(1)}, u32[]{:S(2)}) copy-start(f32[6,3,8]{2,1,0:T(4,128)S(1)} %gather_fusion.4) | copy-start | bytes 1732
  46.9 15.1 %copy-start.14 = (s32[6,8,360]{2,1,0:T(8,128)S(1)}, s32[6,8,360]{2,1,0:T(8,128)}, u32[]{:S(2)}) copy-start(s32[6,8,360]{2,1,0:T(8,128)} %get-tuple-element.144) | copy-start | bytes 207364
  91.6 4.3 collective-permute-start.3
  92.3 5.3 collective-permute-start.2
  281.6 13.6 %copy-start.36 = (f32[6]{0:T(128)S(1)}, f32[6]{0:T(128)}, u32[]{:S(2)}) copy-start(f32[6]{0:T(128)} %gather_fusion.17) | copy-start | bytes 76
  281.6 14.8 %copy-start.27 = (s32[8,360,1]{1,0,2:T(8,128)S(1)}, s32[8,360,1]{1,0,2:T(8,128)}, u32[]{:S(2)}) copy-start(s32[8,360,1]{1,0,2:T(8,128)} %get-tuple-element.135) | copy-start | bytes 34564
  281.6 14.9 %copy-start.13 = (s32[6,8,360]{2,1,0:T(8,128)S(1)}, s32[6,8,360]{2,1,0:T(8,128)}, u32[]{:S(2)}) copy-start(s32[6,8,360]{2,1,0:T(8,128)} %get-tuple-element.143) | copy-start | bytes 207364
  281.6 14.9 %copy-start.23 = (f32[6,3,8]{2,1,0:T(4,128)S(1)}, f32[6,3,8]{2,1,0:T(4,128)}, u32[]{:S(2)}) copy-start(f32[6,3,8]{2,1,0:T(4,128)} %copy-done.22) | copy-start | bytes 1732
  295.1 227.6 %reduce-scatter.3.cloned.1.call-start = ((), (), s32[]{:S(2)}) async-start(), calls=%async_computation.2 | async-start | bytes 3538944 | tf_op jit(solution)/shard_map/reduce_scatter | solution.py:112
  296.5 14.4 %copy-start.12 = (s32[6,8,360]{2,1,0:T(8,128)S(1)}, s32[6,8,360]{2,1,0:T(8,128)}, u32[]{:S(2)}) copy-start(s32[6,8,360]{2,1,0:T(8,128)} %get-tuple-element.142) | copy-start | bytes 207364
  296.5 14.4 %copy-start.33 = (f32[6]{0:T(128)S(1)}, f32[6]{0:T(128)}, u32[]{:S(2)}) copy-start(f32[6]{0:T(128)} %broadcast_subtract_fusion) | copy-start | bytes 76
  310.9 14.1 %copy-start.11 = (s32[6,8,360]{2,1,0:T(8,128)S(1)}, s32[6,8,360]{2,1,0:T(8,128)}, u32[]{:S(2)}) copy-start(s32[6,8,360]{2,1,0:T(8,128)} %get-tuple-element.139) | copy-start | bytes 207364
  325.0 22.0 %copy-start.26 = (s32[8,360,1]{1,0,2:T(8,128)S(1)}, s32[8,360,1]{1,0,2:T(8,128)}, u32[]{:S(2)}) copy-start(s32[8,360,1]{1,0,2:T(8,128)} %get-tuple-element.136) | copy-start | bytes 34564
  325.0 22.1 %copy-start.25 = (s32[8,360,1]{1,0,2:T(8,128)S(1)}, s32[8,360,1]{1,0,2:T(8,128)}, u32[]{:S(2)}) copy-start(s32[8,360,1]{1,0,2:T(8,128)} %get-tuple-element.137) | copy-start | bytes 34564
  325.0 22.2 %copy-start.24 = (s32[8,360,1]{1,0,2:T(8,128)S(1)}, s32[8,360,1]{1,0,2:T(8,128)}, u32[]{:S(2)}) copy-start(s32[8,360,1]{1,0,2:T(8,128)} %get-tuple-element.131) | copy-start | bytes 34564
  340.6 13.8 %collective-permute-start.5 = (bf16[1,360,512]{2,1,0:T(8,128)(2,1)S(1)}, bf16[1,360,512]{2,1,0:T(8,128)(2,1)S(1)}, u32[]{:S(2)}, u32[]{:S(2)}) collective-permute-start(bf16[1,360,512]{2,1,0:T(8,128)(2,1)S(1)} %get-tuple-element.120), channel_id=1, source_target_pairs={{4,0},{8,4},{12,8},{16,12},{20,16},{24,20},{28,24},{5,1},{9,5},{13... | collective-permute-start | bytes 1105928 | tf_op jit(solution)/shard_map/ppermute | solution.py:21
  341.9 20.5 %collective-permute-start.4 = (bf16[1,360,512]{2,1,0:T(8,128)(2,1)S(1)}, bf16[1,360,512]{2,1,0:T(8,128)(2,1)S(1)}, u32[]{:S(2)}, u32[]{:S(2)}) collective-permute-start(bf16[1,360,512]{2,1,0:T(8,128)(2,1)S(1)} %get-tuple-element.119), channel_id=1, source_target_pairs={{0,4},{4,8},{8,12},{12,16},{16,20},{20,24},{24,28},{1,5},{5,9},{9,... | collective-permute-start | bytes 1105928 | tf_op jit(solution)/shard_map/ppermute | solution.py:20
  347.4 16.7 %copy-start.3 = (bf16[6,360,512]{2,1,0:T(8,128)(2,1)S(1)}, bf16[6,360,512]{2,1,0:T(8,128)(2,1)}, u32[]{:S(2)}) copy-start(bf16[6,360,512]{2,1,0:T(8,128)(2,1)} %get-tuple-element.111) | copy-start | bytes 6635524
  354.3 20.4 %copy-start.9 = (bf16[1,360,512]{2,1,0:T(8,128)(2,1)}, bf16[1,360,512]{2,1,0:T(8,128)(2,1)S(1)}, u32[]{:S(2)}) copy-start(bf16[1,360,512]{2,1,0:T(8,128)(2,1)S(1)} %collective-permute-done.5) | copy-start | bytes 1105924
  363.5 11.4 %collective-permute-start.7 = (bf16[8,16,512]{2,1,0:T(8,128)(2,1)S(1)}, bf16[8,16,512]{2,1,0:T(8,128)(2,1)S(1)}, u32[]{:S(2)}, u32[]{:S(2)}) collective-permute-start(bf16[8,16,512]{2,1,0:T(8,128)(2,1)S(1)} %get-tuple-element.116), channel_id=1, source_target_pairs={{1,0},{2,1},{3,2},{0,3},{5,4},{6,5},{7,6},{4,7},{9,8},{10,9},{11,1... | collective-permute-start | bytes 393224 | tf_op jit(solution)/shard_map/ppermute | solution.py:21
  363.8 11.7 %collective-permute-start.6 = (bf16[8,16,512]{2,1,0:T(8,128)(2,1)S(1)}, bf16[8,16,512]{2,1,0:T(8,128)(2,1)}, u32[]{:S(2)}, u32[]{:S(2)}) collective-permute-start(bf16[8,16,512]{2,1,0:T(8,128)(2,1)S(1)} %get-tuple-element.115), channel_id=1, source_target_pairs={{0,1},{1,2},{2,3},{3,0},{4,5},{5,6},{6,7},{7,4},{8,9},{9,10},{10,1... | collective-permute-start | bytes 393224 | tf_op jit(solution)/shard_map/ppermute | solution.py:20
  374.8 170.1 %reduce-scatter.5.cloned.1.call-start = ((), (), s32[]{:S(2)}) async-start(), calls=%async_computation.3 | async-start | bytes 491520 | tf_op jit(solution)/shard_map/reduce_scatter | solution.py:113
  (18 other events, 111.9 us)
Sparse Core Ops, SparseCore 0:
  19.6 46.5 all-gather.4
  295.2 29.1 all-gather.6
  374.9 76.0 reduce-scatter.2
  522.8 21.9 reduce-scatter.4
where the time goes:
time: 560 us; the launch traced here: 552 us
  matrix products  297 us (53%)
  local copies, waits for them, and re-layouts  143 us (26%)
  other arithmetic  54 us (10%)
  waiting for transfers between devices  29.2 us (5%)
  between operations  14.9 us (3%)
  starting transfers between devices  14.1 us (3%)
    dot_general x6, matrix products, near_terms(): jnp.einsum('krjm,rmc->krjc', band, source_rows, precision=lax.Precision.H...  136 us
    dot_general x6, matrix products, near_terms(): jnp.einsum('krs,rsjm->krjm', weights, onehot, precision=lax.Precision.HIG...  88.8 us
    gather x8, local copies, waits for them, and re-layouts, convolve(): picked = cycles[cycle_pos][col_index].astype(jnp.float32)  85.6 us
    dot_general x8, matrix products, convolve(): jnp.einsum('ks,sjc->kjc', weights, picked, precision=lax.Precision.HIGHEST)  40.6 us
    scatter-add x8, other arithmetic, convolve(): summed = summed.at[:, target].add(contrib)  32.4 us
    unnamed x82, local copies, waits for them, and re-layouts  28.5 us
    reduce_scatter x1, waiting for transfers between devices, per_device(): lax.psum_scatter(partial_grad, 'lon', scatter_dimension=2, tiled=True)  12 us
  transfers between devices with their start and end apart: 12, of which 5 were waited for; matrix products, arithmetic and copies ran while one was open for 68% of the time, Pallas kernels for 0%

commit v1 on v0

v1 whole, which is shorter than its diff:
```python
import functools
import math

import jax
import jax.numpy as jnp
import numpy as np
from jax import lax
from jax.experimental import pallas as pl
from jax.experimental.pallas import tpu as pltpu
from jax.sharding import PartitionSpec as P

HALO = 16
POLAR = 1
TJ = 128
WIN = TJ + 2 * HALO
SPAN = 512
F32 = jnp.float32
BF16 = jnp.bfloat16
VMEM_LIMIT = 50 * 1024 * 1024


def widen(shard, padded_width):
    lat, lon = lax.axis_size("lat"), lax.axis_size("lon")
    up = [(i, i + 1) for i in range(lat - 1)]
    down = [(i + 1, i) for i in range(lat - 1)]
    before = lax.ppermute(shard[-1:], "lat", up)
    after = lax.ppermute(shard[:1], "lat", down)
    rows = jnp.concatenate([before, shard, after], axis=0)
    right = [(i, (i + 1) % lon) for i in range(lon)]
    left = [((i + 1) % lon, i) for i in range(lon)]
    west = lax.ppermute(rows[:, -HALO:], "lon", right)
    east = lax.ppermute(rows[:, :HALO], "lon", left)
    fill = padded_width - shard.shape[1]
    parts = [west, rows, east]
    if fill:
        parts.append(jnp.zeros((rows.shape[0], fill, shard.shape[2]), shard.dtype))
    return jnp.concatenate(parts, axis=1)


def base_rows(psi_loc, off_loc, polar_pad, rows, adjoint):
    targets = np.arange(rows)
    places = jnp.arange(SPAN, dtype=jnp.int32)
    total = None
    for d in range(3):
        wrow = targets + (2 - d if adjoint else 1)
        window = 2 - d if adjoint else d
        w = psi_loc[:, wrow, d, :] * (1.0 - polar_pad[wrow])[None, :, None]
        off = off_loc[wrow, d, :]
        off = jnp.clip(-off if adjoint else off, -HALO, HALO) + HALO + window * WIN
        hit = (off[:, :, None] == places[None, None, :]).astype(F32)
        term = jnp.sum(w[..., None] * hit[None], axis=2)
        total = term if total is None else total + term
    total = jnp.transpose(total, (1, 0, 2))
    return jnp.pad(total, ((0, 0), (0, 5), (0, 0)))


def polar_kernel(pairs, ntgt, cycle, blocks, flag_ref, start_ref, w_ref, g_ref, out_ref, buf):
    extra = blocks * TJ
    chans = g_ref.shape[2]

    @pl.when(flag_ref[0] > 0)
    def _():
        for e in range(g_ref.shape[0]):

            @pl.loop(0, cycle // 16)
            def _(i):
                at = pl.multiple_of(i * 16, 16)
                buf[e, pl.ds(at, 16), :] = g_ref[e, pl.ds(at, 16), :].astype(F32)

            @pl.loop(0, extra // 16)
            def _(i):
                at = pl.multiple_of(i * 16, 16)
                buf[e, pl.ds(cycle + at, 16), :] = g_ref[e, pl.ds(at, 16), :].astype(F32)

        for t in range(ntgt):

            @pl.loop(0, extra // 16)
            def _(i):
                at = pl.multiple_of(i * 16, 16)
                acc = [jnp.zeros((16, chans), F32) for _ in range(3)]
                for p, (tgt, e) in enumerate(pairs):
                    if tgt != t:
                        continue
                    for s in range(8):
                        start = start_ref[p * 8 + s]
                        low = pl.multiple_of(start // 8 * 8 + at, 8)
                        x = buf[e, pl.ds(low, 24), :]
                        x = pltpu.roll(x, lax.rem(24 - lax.rem(start, 8), 24), 0)[:16]
                        for k in range(3):
                            acc[k] = acc[k] + w_ref[(p * 3 + k) * 8 + s] * x
                for k in range(3):
                    out_ref[t * 3 + k, pl.ds(at, 16), :] = acc[k]


def polar_terms(gathered, flag, starts, weights, pairs, ntgt, padded_width):
    ns, cycle, chans = gathered.shape
    smem = pl.BlockSpec(memory_space=pltpu.SMEM)
    vmem = pl.BlockSpec(memory_space=pltpu.VMEM)
    return pl.pallas_call(
        functools.partial(polar_kernel, pairs, ntgt, cycle, padded_width // TJ),
        out_shape=jax.ShapeDtypeStruct((ntgt * 3, padded_width, chans), F32),
        in_specs=[smem, smem, smem, vmem],
        out_specs=vmem,
        scratch_shapes=[pltpu.VMEM((ns, cycle + padded_width, chans), F32)],
        compiler_params=pltpu.CompilerParams(vmem_limit_bytes=VMEM_LIMIT),
        name="polar",
    )(flag, starts.reshape(-1), weights.reshape(-1), gathered)


def filter_row(slot_ref, base_ref, srcs, extra_ref, band, src, filt, blocks):
    r = pl.program_id(0)
    chans = src.shape[1]
    src[3 * WIN :, :] = jnp.zeros((SPAN - 3 * WIN, chans), BF16)
    for k in range(3):
        row = jnp.broadcast_to(base_ref[0, k : k + 1, :], (TJ, SPAN))
        moved = pltpu.roll(row, 0, 1, stride=1, stride_axis=0)
        band[k * TJ : (k + 1) * TJ, :] = moved.astype(BF16)
    for b in range(blocks):
        for e in range(3):
            src[e * WIN : (e + 1) * WIN, :] = srcs[e][0, b * TJ : b * TJ + WIN, :]
        acc = jnp.dot(band[...], src[...], preferred_element_type=F32)
        here = slice(b * TJ, (b + 1) * TJ)
        for k in range(3):
            filt[here, k * chans : (k + 1) * chans] = acc[k * TJ : (k + 1) * TJ].astype(BF16)

        @pl.when(slot_ref[r] >= 0)
        def _():
            for k in range(3):
                whole = acc[k * TJ : (k + 1) * TJ] + extra_ref[k, here, :]
                filt[here, k * chans : (k + 1) * chans] = whole.astype(BF16)


def forward_kernel(blocks, slot_ref, base_ref, s0, s1, s2, extra_ref, mix_ref, state_ref, cot_ref,
                   out_ref, slope_ref, filt_ref, band, src):
    width = state_ref.shape[1]
    filt = filt_ref.at[0]
    filter_row(slot_ref, base_ref, (s0, s1, s2), extra_ref, band, src, filt, blocks)
    padded = blocks * TJ
    if padded > width:
        low = width // 16 * 16
        slope_ref[0, low:, :] = jnp.zeros((padded - low, slope_ref.shape[2]), BF16)
    for b in range(blocks):
        at, n = b * TJ, min(TJ, width - b * TJ)
        mixed = jnp.dot(filt[at : at + TJ, :], mix_ref[...], preferred_element_type=F32)[:n]
        rising = 0.5 * (1.0 + lax.erf(mixed * 0.7071067811865476))
        bump = mixed * jnp.exp(-0.5 * mixed * mixed) * 0.3989422804014327
        x = state_ref[0, at : at + n, :].astype(F32)
        g = cot_ref[0, at : at + n, :].astype(F32)
        out_ref[0, at : at + n, :] = (x + mixed * rising).astype(BF16)
        slope_ref[0, at : at + n, :] = (g * (rising + bump)).astype(BF16)


def backward_kernel(blocks, slot_ref, base_ref, s0, s1, s2, extra_ref, mix_ref, cot_ref,
                    grad_ref, band, src, filt):
    width = cot_ref.shape[1]
    filter_row(slot_ref, base_ref, (s0, s1, s2), extra_ref, band, src, filt, blocks)
    back = jnp.dot(filt[...], mix_ref[...], preferred_element_type=F32)[:width]
    grad_ref[0] = (cot_ref[0].astype(F32) + back).astype(BF16)


def grad_kernel(scale, filt_ref, slope_ref, out_ref):
    r = pl.program_id(0)
    term = lax.dot_general(
        filt_ref[0], slope_ref[0], (((0,), (0,)), ((), ())), preferred_element_type=F32
    )

    @pl.when(r == 0)
    def _():
        out_ref[...] = term

    @pl.when(r > 0)
    def _():
        out_ref[...] += term

    @pl.when(r == pl.num_programs(0) - 1)
    def _():
        out_ref[...] *= scale


def conv_specs(wl, padded, chans):
    one = lambda e: pl.BlockSpec((1, wl, chans), lambda r, slot, e=e: (r + e, 0, 0))
    return [
        pl.BlockSpec((1, 8, SPAN), lambda r, slot: (r, 0, 0)),
        one(0),
        one(1),
        one(2),
        pl.BlockSpec((3, padded, chans), lambda r, slot: (jnp.maximum(slot[r], 0), 0, 0)),
        pl.BlockSpec((3 * chans, chans), lambda r, slot: (0, 0)),
    ]


def per_device(state, filter_values, offsets, mixing, cotangent):
    rows, width, chans = state.shape
    nrings = offsets.shape[0]
    nlat, nlon = lax.axis_size("lat"), lax.axis_size("lon")
    cycle = width * nlon
    blocks = -(-width // TJ)
    padded = blocks * TJ
    wl = padded + 2 * HALO
    lat_id = lax.axis_index("lat")
    lat_start = lat_id * rows
    lon_start = lax.axis_index("lon") * width
    psi_pad = jnp.pad(filter_values, ((0, 0), (1, 1), (0, 0), (0, 0)))
    off_pad = jnp.pad(offsets, ((1, 1), (0, 0), (0, 0)))
    psi_loc = lax.dynamic_slice_in_dim(psi_pad, lat_start, rows + 2, 1)
    off_loc = lax.dynamic_slice_in_dim(off_pad, lat_start, rows + 2, 0)
    ring = lat_start + jnp.arange(rows + 2, dtype=jnp.int32) - 1
    polar_pad = ((ring < POLAR) | (ring >= nrings - POLAR)).astype(F32)
    south = lat_id == 0
    north = lat_id == nlat - 1
    flag = (south | north).astype(jnp.int32)[None]
    row_ids = jnp.arange(rows, dtype=jnp.int32)

    w_pole = jnp.where(south, psi_loc[:, 1], psi_loc[:, rows])
    o_pole = jnp.where(south, off_loc[1], off_loc[rows])
    w_two = jnp.where(south, w_pole[:, 1:3], w_pole[:, 0:2])
    o_two = jnp.where(south, o_pole[1:3], o_pole[0:2])
    two = jnp.where(south, state[:2], state[-2:])
    gathered = lax.all_gather(two, "lon", axis=1, tiled=True)
    wide = widen(state, padded)
    fwd_extra = polar_terms(
        gathered, flag, (lon_start + o_two) % cycle, jnp.transpose(w_two, (1, 0, 2)),
        [(0, 0), (0, 1)], 1, padded,
    )
    fwd_slot = jnp.where((south & (row_ids == 0)) | (north & (row_ids == rows - 1)), 0, -1).astype(jnp.int32)
    fwd_base = base_rows(psi_loc, off_loc, polar_pad, rows, False)
    field = pl.BlockSpec((1, width, chans), lambda r, slot: (r, 0, 0))
    params = pltpu.CompilerParams(vmem_limit_bytes=VMEM_LIMIT)
    flops = rows * padded * chans * (3 * SPAN + 3 * chans) * 2
    cost = pl.CostEstimate(flops=flops, bytes_accessed=rows * padded * chans * 20, transcendentals=0)
    output, slope, filtered = pl.pallas_call(
        functools.partial(forward_kernel, blocks),
        out_shape=(
            jax.ShapeDtypeStruct(state.shape, BF16),
            jax.ShapeDtypeStruct((rows, padded, chans), BF16),
            jax.ShapeDtypeStruct((rows, padded, 3 * chans), BF16),
        ),
        grid_spec=pltpu.PrefetchScalarGridSpec(
            num_scalar_prefetch=1,
            grid=(rows,),
            in_specs=conv_specs(wl, padded, chans) + [field, field],
            out_specs=(
                field,
                pl.BlockSpec((1, padded, chans), lambda r, slot: (r, 0, 0)),
                pl.BlockSpec((1, padded, 3 * chans), lambda r, slot: (r, 0, 0)),
            ),
            scratch_shapes=[pltpu.VMEM((3 * TJ, SPAN), BF16), pltpu.VMEM((SPAN, chans), BF16)],
        ),
        compiler_params=params,
        cost_estimate=cost,
        name="forward",
    )(fwd_slot, fwd_base, wide, wide, wide, fwd_extra, mixing.reshape(3 * chans, chans), state, cotangent)

    local_grad = pl.pallas_call(
        functools.partial(grad_kernel, 1.0 / math.sqrt(nrings * cycle)),
        out_shape=jax.ShapeDtypeStruct((3 * chans, chans), F32),
        grid=(rows,),
        in_specs=[
            pl.BlockSpec((1, padded, 3 * chans), lambda r: (r, 0, 0)),
            pl.BlockSpec((1, padded, chans), lambda r: (r, 0, 0)),
        ],
        out_specs=pl.BlockSpec((3 * chans, chans), lambda r: (0, 0)),
        compiler_params=params,
        cost_estimate=cost,
        name="channel_grad",
    )(filtered, slope).reshape(3, chans, chans)
    partial_grad = lax.psum_scatter(local_grad, "lat", scatter_dimension=1, tiled=True)
    mixing_grad = lax.psum_scatter(partial_grad, "lon", scatter_dimension=2, tiled=True)

    slope = slope[:, :width]
    pole_slope = jnp.where(south, slope[:1], slope[-1:])
    pole_cycle = lax.all_gather(pole_slope, "lon", axis=1, tiled=True)
    slope_wide = widen(slope, padded)
    bwd_extra = polar_terms(
        pole_cycle, flag, (lon_start - o_two[::1]) % cycle, jnp.transpose(w_two, (1, 0, 2)),
        [(0, 0), (1, 0)], 2, padded,
    )
    first = jnp.where(south, 0, rows - 2)
    bwd_slot = jnp.where(
        flag[0] * ((row_ids >= first) & (row_ids < first + 2)) > 0, row_ids - first, -1
    ).astype(jnp.int32)
    bwd_base = base_rows(psi_loc, off_loc, polar_pad, rows, True)
    state_grad = pl.pallas_call(
        functools.partial(backward_kernel, blocks),
        out_shape=jax.ShapeDtypeStruct(state.shape, BF16),
        grid_spec=pltpu.PrefetchScalarGridSpec(
            num_scalar_prefetch=1,
            grid=(rows,),
            in_specs=conv_specs(wl, padded, chans) + [field],
            out_specs=field,
            scratch_shapes=[
                pltpu.VMEM((3 * TJ, SPAN), BF16),
                pltpu.VMEM((SPAN, chans), BF16),
                pltpu.VMEM((padded, 3 * chans), BF16),
            ],
        ),
        compiler_params=params,
        cost_estimate=cost,
        name="backward",
    )(bwd_slot, bwd_base, slope_wide, slope_wide, slope_wide, bwd_extra,
      jnp.swapaxes(mixing, 1, 2).reshape(3 * chans, chans), cotangent)
    return (output, mixing_grad, state_grad)


def solution(mesh):
    in_specs = (P("lat", "lon", None), P(), P(), P(), P("lat", "lon", None))
    out_specs = (P("lat", "lon", None), P(None, "lat", "lon"), P("lat", "lon", None))
    return jax.shard_map(
        per_device, mesh=mesh, in_specs=in_specs, out_specs=out_specs, check_vma=False
    )
```

time: 560 us -> 228 us (0.41); the launches traced: 552 us -> 228 us
  matrix products: 297 us -> 0 us
  local copies, waits for them, and re-layouts: 143 us -> 18.6 us
  waiting for transfers between devices: 29.2 us -> 103 us
  Pallas kernels: 0 us -> 63.8 us
  other arithmetic: 54 us -> 13.8 us
    dot_general x23 -> x0, matrix products: 297 us -> none  [the longest x6 136 us: near_terms(): jnp.einsum('krjm,rmc->krjc', band, source_rows, precision=lax.Precision.H...]
    gather x23 -> x13, local copies, waits for them, and re-layouts: 103 us -> 7.9 us  [the longest x8 4.97 us: base_rows(): w = psi_loc[:, wrow, d, :] * (1.0 - polar_pad[wrow])[None, :, None]]
    pallas_call x0 -> x5, Pallas kernels: none -> 63.8 us  [the longest x2 19.2 us: polar_terms(): pl.pallas_call(functools.partial(polar_kernel, pairs, ntgt, cycle, padded...]
    reduce_scatter x1, waiting for transfers between devices: 0.01 us -> 57.6 us  [per_device(): lax.psum_scatter(local_grad, 'lat', scatter_dimension=1, tiled=True)]
    scatter-add x8 -> x0, other arithmetic: 32.4 us -> none  [convolve(): summed = summed.at[:, target].add(contrib)]
    all_gather x2, waiting for transfers between devices: 0.01 us -> 21.1 us  [the longest x1 16.5 us: per_device(): pole_cycle = lax.all_gather(pole_slope, 'lon', axis=1, tiled=True)]
    unnamed x82 -> x42, local copies, waits for them, and re-layouts: 28.5 us -> 7.53 us
    reduce_scatter x1, waiting for transfers between devices: 12 us -> 0.01 us  [per_device(): lax.psum_scatter(partial_grad, 'lon', scatter_dimension=2, tiled=True)]
  transfers between devices with their start and end apart: 12 -> 12, of which waited for: 5 -> 8; matrix products, arithmetic and copies ran while one was open for 68% -> 11% of each run, Pallas kernels for 0% -> 11%
where the time goes in v1:
time: 228 us
  waiting for transfers between devices  103 us (45%)
  Pallas kernels  63.8 us (28%)
  local copies, waits for them, and re-layouts  18.6 us (8%)
  between operations  14.3 us (6%)
  starting transfers between devices  14 us (6%)
  other arithmetic  13.8 us (6%)
    reduce_scatter x1, waiting for transfers between devices, per_device(): lax.psum_scatter(local_grad, 'lat', scatter_dimension=1, tiled=True)  57.6 us
    pallas_call x2, Pallas kernels, polar_terms(): pl.pallas_call(functools.partial(polar_kernel, pairs, ntgt, cycle, padded...  19.2 us
    pallas_call x1, Pallas kernels, per_device(): pl.pallas_call(functools.partial(forward_kernel, blocks), out_shape=(jax....  17.7 us
    all_gather x1, waiting for transfers between devices, per_device(): pole_cycle = lax.all_gather(pole_slope, 'lon', axis=1, tiled=True)  16.5 us
    pallas_call x1, Pallas kernels, per_device(): pl.pallas_call(functools.partial(backward_kernel, blocks), out_shape=jax....  15.8 us
    pallas_call x1, Pallas kernels, per_device(): pl.pallas_call(functools.partial(grad_kernel, 1.0 / math.sqrt(nrings * cy...  11.1 us
    ppermute x2, starting transfers between devices, widen(): before = lax.ppermute(shard[-1:], 'lat', up)  10.2 us
    ppermute x2, waiting for transfers between devices, widen(): after = lax.ppermute(shard[:1], 'lat', down)  9.74 us
  transfers between devices with their start and end apart: 12, of which 8 were waited for; matrix products, arithmetic and copies ran while one was open for 11% of the time, Pallas kernels for 11%

profile of v1, /device:TPU:0, one launch (start us, length us, event | category | flops | bytes accessed | tf_op | source)
XLA Modules:
  0.0 227.6 jit_solution(3748537796911038971)
XLA Ops:
  7.3 1.9 fusion.11
  9.2 5.6 %collective-permute-start = (bf16[1,360,512]{2,1,0:T(8,128)(2,1)}, bf16[1,360,512]{2,1,0:T(8,128)(2,1)}, u32[]{:S(2)}, u32[]{:S(2)}) collective-permute-start(bf16[1,360,512]{2,1,0:T(8,128)(2,1)} %get-tuple-element.21), channel_id=1, source_target_pairs={{0,4},{4,8},{8,12},{12,16},{16,20},{20,24},{24,28},{1,5},{5,9},{9,... | collective-permute-start | bytes 1105928 | tf_op jit(solution)/shard_map/ppermute | solution.py:26
  14.8 1.3 collective-permute-start.1
  16.1 2.4 %slice_select_fusion = bf16[2,360,512]{2,1,0:T(8,128)(2,1)} fusion(bf16[6,360,512]{2,1,0:T(8,128)(2,1)} %state_ref.1, pred[]{:T(512)S(6)} %eq.117), kind=kLoop, calls=%fused_computation.15 | loop fusion | flops 368640 | bytes 2211841 | tf_op jit(solution)/shard_map/jit(_where)/select_n | solution.py:218
  22.6 0.6 gather_fusion.1
  24.3 5.7 %collective-permute-done = bf16[1,360,512]{2,1,0:T(8,128)(2,1)} collective-permute-done((bf16[1,360,512]{2,1,0:T(8,128)(2,1)}, bf16[1,360,512]{2,1,0:T(8,128)(2,1)}, u32[]{:S(2)}, u32[]{:S(2)}) %collective-permute-start) | collective-permute-done | bytes 368672 | tf_op jit(solution)/shard_map/ppermute | solution.py:26
  30.1 1.0 constant_dynamic-update-slice_fusion.2
  31.3 1.6 copy-done.9
  33.8 5.7 %collective-permute-done.3 = bf16[8,16,512]{2,1,0:T(8,128)(2,1)S(1)} collective-permute-done((bf16[8,16,512]{2,1,0:T(8,128)(2,1)S(1)}, bf16[8,16,512]{2,1,0:T(8,128)(2,1)S(1)}, u32[]{:S(2)}, u32[]{:S(2)}) %collective-permute-start.3) | collective-permute-done | bytes 131104 | tf_op jit(solution)/shard_map/ppermute | solution.py:32
  39.4 2.2 collective-permute-done.2
  41.6 4.3 %maximum_maximum_fusion.s0.s1.s2 = bf16[8,416,512]{2,1,0:T(8,128)(2,1)} fusion(bf16[8,16,512]{2,1,0:T(8,128)(2,1)S(1)} %collective-permute-done.3, bf16[8,360,512]{2,1,0:T(8,128)(2,1)} %copy-done.9, bf16[8,16,512]{2,1,0:T(8,128)(2,1)S(1)} %collective-permute-done.2, bf16[416]{0:T(512)(128)(2,1)S(1)} %pad.43.clone), kind=kLoop, calls=%fused_computation.13 | loop fusion | flops 13631488 | bytes 6619968 | tf_op jit(solution)/shard_map/concatenate | solution.py:37
  45.9 4.6 %all-gather.3.cloned.1.call-done.g_ref = bf16[2,1440,512]{2,1,0:T(8,128)(2,1)} async-done(((bf16[2,360,512]{2,1,0:T(8,128)(2,1)}), bf16[2,1440,512]{2,1,0:T(8,128)(2,1)}) %all-gather.3.cloned.1.call-update) | async-done | bytes 2949136 | tf_op jit(solution)/shard_map/all_gather | solution.py:219
  50.6 9.6 %polar.2.extra_ref = f32[3,384,512]{2,1,0:T(8,128)S(1)} custom-call(s32[1]{0:T(128)} %bitcast.4.flag_ref, s32[16]{0:T(128)S(1)} %reshape.128.start_ref, f32[48]{0:T(128)S(1)} %reshape.129.w_ref, bf16[2,1440,512]{2,1,0:T(8,128)(2,1)} %all-gather.3.cloned.1.call-done.g_ref), custom_call_target="tpu_custom_call" | custom-call | tf_op jit(solution)/shard_map/polar/pallas_call | solution.py:99
  60.2 1.4 copy-done.3
  61.5 17.7 %forward.1 = (bf16[6,360,512]{2,1,0:T(8,128)(2,1)}, bf16[6,384,512]{2,1,0:T(8,128)(2,1)}, bf16[6,384,1536]{2,1,0:T(8,128)(2,1)}) custom-call(s32[6]{0:T(128)S(1)} %or_select_fusion.slot_ref, f32[6,8,512]{2,1,0:T(8,128)S(1)} %pad.29.base_ref, bf16[8,416,512]{2,1,0:T(8,128)(2,1)} %maximum_maximum_fusion.s0.s1.s2, ...), custom_call_target="tpu_custom_call" | custom-call | flops 7247757312 | bytes 23592960 | tf_op jit(solution)/shard_map/forward/pallas_call | solution.py:231
  79.3 1.7 copy-done.1
  80.9 11.1 %channel_grad.1 = f32[1536,512]{1,0:T(8,128)} custom-call(bf16[6,384,1536]{2,1,0:T(8,128)(2,1)} %get-tuple-element.7.filt_ref, bf16[6,384,512]{2,1,0:T(8,128)(2,1)S(1)} %copy-done.1), custom_call_target="tpu_custom_call" | custom-call | flops 7247757312 | bytes 23592960 | tf_op jit(solution)/shard_map/channel_grad/pallas_call | solution.py:254
  94.6 0.6 gather_fusion.11
  95.2 0.6 gather_fusion.8
  96.0 1.0 broadcast_select_fusion
  97.3 1.3 collective-permute-start.5
  98.6 4.6 %collective-permute-start.4 = (bf16[1,360,512]{2,1,0:T(8,128)(2,1)}, bf16[1,360,512]{2,1,0:T(8,128)(2,1)S(1)}, u32[]{:S(2)}, u32[]{:S(2)}) collective-permute-start(bf16[1,360,512]{2,1,0:T(8,128)(2,1)} %get-tuple-element.19), channel_id=1, source_target_pairs={{0,4},{4,8},{8,12},{12,16},{16,20},{20,24},{24,28},{1,5},{5,9},{9,... | collective-permute-start | bytes 1105928 | tf_op jit(solution)/shard_map/ppermute | solution.py:26
  103.8 9.7 %collective-permute-done.5 = bf16[1,360,512]{2,1,0:T(8,128)(2,1)S(1)} collective-permute-done((bf16[1,360,512]{2,1,0:T(8,128)(2,1)}, bf16[1,360,512]{2,1,0:T(8,128)(2,1)S(1)}, u32[]{:S(2)}, u32[]{:S(2)}) %collective-permute-start.5) | collective-permute-done | bytes 368672 | tf_op jit(solution)/shard_map/ppermute | solution.py:27
  113.5 1.0 collective-permute-done.4
  114.5 0.8 pad_maximum_fusion.2
  115.9 0.7 copy.79
  116.6 57.6 %reduce-scatter.3.cloned.1.call-done = f32[3,64,512]{2,1,0:T(8,128)} async-done(((f32[3,512,512]{2,1,0:T(8,128)}), f32[3,64,512]{2,1,0:T(8,128)}) %reduce-scatter.3.cloned.1.call-update) | async-done | bytes 393232 | tf_op jit(solution)/shard_map/reduce_scatter | solution.py:267
  174.3 3.5 %maximum_maximum_fusion.1.s0.s1.s2 = bf16[8,416,512]{2,1,0:T(8,128)(2,1)} fusion(bf16[8,16,512]{2,1,0:T(8,128)(2,1)S(1)} %collective-permute-done.7, bf16[1,360,512]{2,1,0:T(8,128)(2,1)} %copy-done.10, bf16[6,360,512]{2,1,0:T(8,128)(2,1)} %copy-done.8, bf16[1,360,512]{2,1,0:T(8,128)(2,1)} %copy-done.11, bf16[8,16,512]{2,1,0:T(8,128)(2,1)} %collective-permute-done.6, ...), kind=kLoop, calls=%fused_computation.14 | loop fusion | flops 20447232 | bytes 6619968 | tf_op jit(solution)/shard_map/concatenate | solution.py:37
  177.8 16.5 %all-gather.5.cloned.1.call-done.g_ref = bf16[1,1440,512]{2,1,0:T(8,128)(2,1)} async-done(((bf16[1,360,512]{2,1,0:T(8,128)(2,1)}), bf16[1,1440,512]{2,1,0:T(8,128)(2,1)}) %all-gather.5.cloned.1.call-update) | async-done | bytes 1474576 | tf_op jit(solution)/shard_map/all_gather | solution.py:272
  194.3 1.4 copy-done.6
  195.6 9.6 %polar.3.extra_ref = f32[6,384,512]{2,1,0:T(8,128)} custom-call(s32[1]{0:T(128)} %bitcast.4.flag_ref, s32[16]{0:T(128)S(1)} %reshape.132.start_ref, f32[48]{0:T(128)S(1)} %reshape.129.w_ref, bf16[1,1440,512]{2,1,0:T(8,128)(2,1)S(1)} %copy-done.6), custom_call_target="tpu_custom_call" | custom-call | tf_op jit(solution)/shard_map/polar/pallas_call | solution.py:99
  205.3 15.8 %backward.1 = bf16[6,360,512]{2,1,0:T(8,128)(2,1)} custom-call(s32[6]{0:T(128)S(1)} %compare_select_fusion.slot_ref, f32[6,8,512]{2,1,0:T(8,128)S(1)} %pad.30.base_ref, bf16[8,416,512]{2,1,0:T(8,128)(2,1)} %maximum_maximum_fusion.1.s0.s1.s2, bf16[8,416,512]{2,1,0:T(8,128)(2,1)} %maximum_maximum_fusion.1.s0.s1.s2, ...), custom_call_target="tpu_custom_call" | custom-call | flops 7247757312 | bytes 23592960 | tf_op jit(solution)/shard_map/backward/pallas_call | solution.py:283
  (120 shorter events, 10.1 us)
Async XLA Ops:
  7.2 11.8 %copy-start.13 = (s32[6]{0:T(128)S(1)}, s32[6]{0:T(128)}, u32[]{:S(2)}) copy-start(s32[6]{0:T(128)} %constant.262) | copy-start | bytes 76
  7.2 12.4 %copy-start.16 = (s32[6]{0:T(128)S(1)}, s32[6]{0:T(128)}, u32[]{:S(2)}) copy-start(s32[6]{0:T(128)} %constant.295) | copy-start | bytes 76
  7.2 14.2 %copy-start.15 = (s32[6]{0:T(128)S(1)}, s32[6]{0:T(128)}, u32[]{:S(2)}) copy-start(s32[6]{0:T(128)} %constant.279) | copy-start | bytes 76
  7.2 11.4 %copy-start.18 = (s32[48,3,8]{0,2,1:T(8,128)S(1)}, s32[48,3,8]{0,2,1:T(8,128)}, u32[]{:S(2)}) copy-start(s32[48,3,8]{0,2,1:T(8,128)} %param.31) | copy-start | bytes 13828
  7.2 11.5 %copy-start.17 = (f32[3,48,3,8]{1,3,2,0:T(8,128)S(1)}, f32[3,48,3,8]{1,3,2,0:T(8,128)}, u32[]{:S(2)}) copy-start(f32[3,48,3,8]{1,3,2,0:T(8,128)} %param.30) | copy-start | bytes 41476
  7.2 43.4 %all-gather.3.cloned.1.call-start = ((), (), s32[]{:S(2)}) async-start(), calls=%async_computation.2 | async-start | bytes 3686400 | tf_op jit(solution)/shard_map/all_gather | solution.py:219
  9.2 20.9 %collective-permute-start = (bf16[1,360,512]{2,1,0:T(8,128)(2,1)}, bf16[1,360,512]{2,1,0:T(8,128)(2,1)}, u32[]{:S(2)}, u32[]{:S(2)}) collective-permute-start(bf16[1,360,512]{2,1,0:T(8,128)(2,1)} %get-tuple-element.21), channel_id=1, source_target_pairs={{0,4},{4,8},{8,12},{12,16},{16,20},{20,24},{24,28},{1,5},{5,9},{9,... | collective-permute-start | bytes 1105928 | tf_op jit(solution)/shard_map/ppermute | solution.py:26
  14.8 16.5 %collective-permute-start.1 = (bf16[1,360,512]{2,1,0:T(8,128)(2,1)S(1)}, bf16[1,360,512]{2,1,0:T(8,128)(2,1)S(1)}, u32[]{:S(2)}, u32[]{:S(2)}) collective-permute-start(bf16[1,360,512]{2,1,0:T(8,128)(2,1)S(1)} %get-tuple-element.20), channel_id=1, source_target_pairs={{4,0},{8,4},{12,8},{16,12},{20,16},{24,20},{28,24},{5,1},{9,5},{13... | collective-permute-start | bytes 1105928 | tf_op jit(solution)/shard_map/ppermute | solution.py:27
  16.1 15.0 %copy-start = (bf16[6,360,512]{2,1,0:T(8,128)(2,1)S(1)}, bf16[6,360,512]{2,1,0:T(8,128)(2,1)}, u32[]{:S(2)}) copy-start(bf16[6,360,512]{2,1,0:T(8,128)(2,1)} %state_ref.1) | copy-start | bytes 6635524
  18.5 155.7 %reduce-scatter.3.cloned.1.call-start = ((), (), s32[]{:S(2)}) async-start(), calls=%async_computation.3 | async-start | bytes 3538944 | tf_op jit(solution)/shard_map/reduce_scatter | solution.py:267
  31.3 1.6 copy-start.9
  32.9 6.5 %collective-permute-start.3 = (bf16[8,16,512]{2,1,0:T(8,128)(2,1)S(1)}, bf16[8,16,512]{2,1,0:T(8,128)(2,1)S(1)}, u32[]{:S(2)}, u32[]{:S(2)}) collective-permute-start(bf16[8,16,512]{2,1,0:T(8,128)(2,1)S(1)} %get-tuple-element.16), channel_id=1, source_target_pairs={{1,0},{2,1},{3,2},{0,3},{5,4},{6,5},{7,6},{4,7},{9,8},{10,9},{11,1... | collective-permute-start | bytes 393224 | tf_op jit(solution)/shard_map/ppermute | solution.py:32
  33.1 8.6 %collective-permute-start.2 = (bf16[8,16,512]{2,1,0:T(8,128)(2,1)S(1)}, bf16[8,16,512]{2,1,0:T(8,128)(2,1)S(1)}, u32[]{:S(2)}, u32[]{:S(2)}) collective-permute-start(bf16[8,16,512]{2,1,0:T(8,128)(2,1)S(1)} %get-tuple-element.15), channel_id=1, source_target_pairs={{0,1},{1,2},{2,3},{3,0},{4,5},{5,6},{6,7},{7,4},{8,9},{9,10},{10,1... | collective-permute-start | bytes 393224 | tf_op jit(solution)/shard_map/ppermute | solution.py:31
  50.6 11.0 %copy-start.4 = (bf16[3,512,512]{2,1,0:T(8,128)(2,1)S(1)}, bf16[3,512,512]{2,1,0:T(8,128)(2,1)}, u32[]{:S(2)}) copy-start(bf16[3,512,512]{2,1,0:T(8,128)(2,1)} %param.32) | copy-start | bytes 4718596
  60.1 1.4 copy-start.3
  79.3 1.7 copy-start.1
  80.9 11.2 %copy-start.14 = (s32[6]{0:T(128)S(1)}, s32[6]{0:T(128)}, u32[]{:S(2)}) copy-start(s32[6]{0:T(128)} %constant.328) | copy-start | bytes 76
  80.9 12.4 %copy-start.12 = (s32[6]{0:T(128)S(1)}, s32[6]{0:T(128)}, u32[]{:S(2)}) copy-start(s32[6]{0:T(128)} %constant.311) | copy-start | bytes 76
  92.1 3.9 %copy-start.2 = (bf16[6,384,512]{2,1,0:T(8,128)(2,1)S(1)}, bf16[6,384,512]{2,1,0:T(8,128)(2,1)}, u32[]{:S(2)}) copy-start(bf16[6,384,512]{2,1,0:T(8,128)(2,1)} %get-tuple-element.8.slope_ref) | copy-start | bytes 7077892
  92.1 102.2 %all-gather.5.cloned.1.call-start = ((), (), s32[]{:S(2)}) async-start(), calls=%async_computation.5 | async-start | bytes 1843200 | tf_op jit(solution)/shard_map/all_gather | solution.py:272
  97.0 124.0 %reduce-scatter.5.cloned.1.call-start = ((), (), s32[]{:S(2)}) async-start(), calls=%async_computation.4 | async-start | bytes 491520 | tf_op jit(solution)/shard_map/reduce_scatter | solution.py:268
  97.3 16.2 %collective-permute-start.5 = (bf16[1,360,512]{2,1,0:T(8,128)(2,1)}, bf16[1,360,512]{2,1,0:T(8,128)(2,1)S(1)}, u32[]{:S(2)}, u32[]{:S(2)}) collective-permute-start(bf16[1,360,512]{2,1,0:T(8,128)(2,1)} %get-tuple-element.18), channel_id=1, source_target_pairs={{4,0},{8,4},{12,8},{16,12},{20,16},{24,20},{28,24},{5,1},{9,5},{13... | collective-permute-start | bytes 1105928 | tf_op jit(solution)/shard_map/ppermute | solution.py:27
  98.6 15.8 %collective-permute-start.4 = (bf16[1,360,512]{2,1,0:T(8,128)(2,1)}, bf16[1,360,512]{2,1,0:T(8,128)(2,1)S(1)}, u32[]{:S(2)}, u32[]{:S(2)}) collective-permute-start(bf16[1,360,512]{2,1,0:T(8,128)(2,1)} %get-tuple-element.19), channel_id=1, source_target_pairs={{0,4},{4,8},{8,12},{12,16},{16,20},{20,24},{24,28},{1,5},{5,9},{9,... | collective-permute-start | bytes 1105928 | tf_op jit(solution)/shard_map/ppermute | solution.py:26
  103.8 10.7 %copy-start.8 = (bf16[6,360,512]{2,1,0:T(8,128)(2,1)}, bf16[6,360,512]{2,1,0:T(8,128)(2,1)S(1)}, u32[]{:S(2)}) copy-start(bf16[6,360,512]{2,1,0:T(8,128)(2,1)S(1)} %slice.78) | copy-start | bytes 6635524
  103.8 12.1 %copy-start.5 = (bf16[3,512,512]{2,1,0:T(8,128)(2,1)S(1)}, bf16[3,512,512]{2,1,0:T(8,128)(2,1)}, u32[]{:S(2)}) copy-start(bf16[3,512,512]{2,1,0:T(8,128)(2,1)} %param.32) | copy-start | bytes 4718596
  113.5 1.7 copy-start.10
  114.5 0.8 copy-start.11
  115.3 59.0 %collective-permute-start.7 = (bf16[8,16,512]{2,1,0:T(8,128)(2,1)}, bf16[8,16,512]{2,1,0:T(8,128)(2,1)S(1)}, u32[]{:S(2)}, u32[]{:S(2)}) collective-permute-start(bf16[8,16,512]{2,1,0:T(8,128)(2,1)} %get-tuple-element.14), channel_id=1, source_target_pairs={{1,0},{2,1},{3,2},{0,3},{5,4},{6,5},{7,6},{4,7},{9,8},{10,9},{11,1... | collective-permute-start | bytes 393224 | tf_op jit(solution)/shard_map/ppermute | solution.py:32
  115.4 58.9 %collective-permute-start.6 = (bf16[8,16,512]{2,1,0:T(8,128)(2,1)}, bf16[8,16,512]{2,1,0:T(8,128)(2,1)}, u32[]{:S(2)}, u32[]{:S(2)}) collective-permute-start(bf16[8,16,512]{2,1,0:T(8,128)(2,1)} %get-tuple-element.13), channel_id=1, source_target_pairs={{0,1},{1,2},{2,3},{3,0},{4,5},{5,6},{6,7},{7,4},{8,9},{9,10},{10,1... | collective-permute-start | bytes 393224 | tf_op jit(solution)/shard_map/ppermute | solution.py:31
  194.3 1.4 copy-start.6
  195.6 9.6 %copy-start.7 = (bf16[6,360,512]{2,1,0:T(8,128)(2,1)S(1)}, bf16[6,360,512]{2,1,0:T(8,128)(2,1)}, u32[]{:S(2)}) copy-start(bf16[6,360,512]{2,1,0:T(8,128)(2,1)} %cot_ref.3) | copy-start | bytes 6635524
Sparse Core Ops, SparseCore 0:
  18.6 31.8 all-gather.2
  92.2 81.9 reduce-scatter.2
  175.8 18.4 all-gather.4
  197.2 20.8 reduce-scatter.4

commit v2 on v1

--- a/solution.py
+++ b/solution.py
@@ -37,6 +37,33 @@
     return jnp.concatenate(parts, axis=1)
 
 
+def scatter_sum(local):
+    k, chans, _ = local.shape
+    nlat, nlon = lax.axis_size("lat"), lax.axis_size("lon")
+    left = local.reshape(k, nlat, chans // nlat, nlon, chans // nlon)
+    left = jnp.transpose(left, (3, 1, 0, 2, 4))
+    for dim, axis in enumerate(("lon", "lat")):
+        count = lax.axis_size(axis)
+        index = lax.axis_index(axis)
+        if count & (count - 1):
+            left = lax.psum_scatter(left, axis, scatter_dimension=dim, tiled=True)
+            left = lax.squeeze(left, (dim,)) if dim == 0 else left[0]
+            continue
+        step = 1
+        while step < count:
+            halves = left.reshape((left.shape[0] // 2, 2) + left.shape[1:])
+            bit = index // step % 2
+            mine = lax.dynamic_index_in_dim(halves, bit, 1, keepdims=False)
+            theirs = lax.dynamic_index_in_dim(halves, 1 - bit, 1, keepdims=False)
+            if (axis == "lon") == (step > 1):
+                theirs = theirs.astype(BF16)
+            got = lax.ppermute(theirs, axis, [(i, i ^ step) for i in range(count)])
+            left = mine + got.astype(F32)
+            step *= 2
+        left = left[0]
+    return left
+
+
 def base_rows(psi_loc, off_loc, polar_pad, rows, adjoint):
     targets = np.arange(rows)
     places = jnp.arange(SPAN, dtype=jnp.int32)
@@ -107,8 +134,8 @@
     )(flag, starts.reshape(-1), weights.reshape(-1), gathered)
 
 
-def filter_row(slot_ref, base_ref, srcs, extra_ref, band, src, filt, blocks):
-    r = pl.program_id(0)
+def filter_row(at, slot_ref, base_ref, srcs, extra_ref, band, src, filt, blocks):
+    r = pl.program_id(0) + at
     chans = src.shape[1]
     src[3 * WIN :, :] = jnp.zeros((SPAN - 3 * WIN, chans), BF16)
     for k in range(3):
@@ -134,11 +161,7 @@
                    out_ref, slope_ref, filt_ref, band, src):
     width = state_ref.shape[1]
     filt = filt_ref.at[0]
-    filter_row(slot_ref, base_ref, (s0, s1, s2), extra_ref, band, src, filt, blocks)
-    padded = blocks * TJ
-    if padded > width:
-        low = width // 16 * 16
-        slope_ref[0, low:, :] = jnp.zeros((padded - low, slope_ref.shape[2]), BF16)
+    filter_row(0, slot_ref, base_ref, (s0, s1, s2), extra_ref, band, src, filt, blocks)
     for b in range(blocks):
         at, n = b * TJ, min(TJ, width - b * TJ)
         mixed = jnp.dot(filt[at : at + TJ, :], mix_ref[...], preferred_element_type=F32)[:n]
@@ -150,10 +173,10 @@
         slope_ref[0, at : at + n, :] = (g * (rising + bump)).astype(BF16)
 
 
-def backward_kernel(blocks, slot_ref, base_ref, s0, s1, s2, extra_ref, mix_ref, cot_ref,
-                    grad_ref, band, src, filt):
+def backward_kernel(blocks, at, slot_ref, base_ref, s0, s1, s2, extra_ref, mix_ref, cot_ref, *rest):
+    grad_ref, band, src, filt = rest[-4:]
     width = cot_ref.shape[1]
-    filter_row(slot_ref, base_ref, (s0, s1, s2), extra_ref, band, src, filt, blocks)
+    filter_row(at, slot_ref, base_ref, (s0, s1, s2), extra_ref, band, src, filt, blocks)
     back = jnp.dot(filt[...], mix_ref[...], preferred_element_type=F32)[:width]
     grad_ref[0] = (cot_ref[0].astype(F32) + back).astype(BF16)
 
@@ -161,7 +184,7 @@
 def grad_kernel(scale, filt_ref, slope_ref, out_ref):
     r = pl.program_id(0)
     term = lax.dot_general(
-        filt_ref[0], slope_ref[0], (((0,), (0,)), ((), ())), preferred_element_type=F32
+        filt_ref[0, : slope_ref.shape[1], :], slope_ref[0], (((0,), (0,)), ((), ())), preferred_element_type=F32
     )
 
     @pl.when(r == 0)
@@ -177,14 +200,14 @@
         out_ref[...] *= scale
 
 
-def conv_specs(wl, padded, chans):
-    one = lambda e: pl.BlockSpec((1, wl, chans), lambda r, slot, e=e: (r + e, 0, 0))
+def conv_specs(wl, padded, chans, at=0):
+    one = lambda e: pl.BlockSpec((1, wl, chans), lambda r, slot, e=e: (r + at + e, 0, 0))
     return [
-        pl.BlockSpec((1, 8, SPAN), lambda r, slot: (r, 0, 0)),
+        pl.BlockSpec((1, 8, SPAN), lambda r, slot: (r + at, 0, 0)),
         one(0),
         one(1),
         one(2),
-        pl.BlockSpec((3, padded, chans), lambda r, slot: (jnp.maximum(slot[r], 0), 0, 0)),
+        pl.BlockSpec((3, padded, chans), lambda r, slot: (jnp.maximum(slot[r + at], 0), 0, 0)),
         pl.BlockSpec((3 * chans, chans), lambda r, slot: (0, 0)),
     ]
 
@@ -232,7 +255,7 @@
         functools.partial(forward_kernel, blocks),
         out_shape=(
             jax.ShapeDtypeStruct(state.shape, BF16),
-            jax.ShapeDtypeStruct((rows, padded, chans), BF16),
+            jax.ShapeDtypeStruct(state.shape, BF16),
             jax.ShapeDtypeStruct((rows, padded, 3 * chans), BF16),
         ),
         grid_spec=pltpu.PrefetchScalarGridSpec(
@@ -241,7 +264,7 @@
             in_specs=conv_specs(wl, padded, chans) + [field, field],
             out_specs=(
                 field,
-                pl.BlockSpec((1, padded, chans), lambda r, slot: (r, 0, 0)),
+                field,
                 pl.BlockSpec((1, padded, 3 * chans), lambda r, slot: (r, 0, 0)),
             ),
             scratch_shapes=[pltpu.VMEM((3 * TJ, SPAN), BF16), pltpu.VMEM((SPAN, chans), BF16)],
@@ -257,22 +280,20 @@
         grid=(rows,),
         in_specs=[
             pl.BlockSpec((1, padded, 3 * chans), lambda r: (r, 0, 0)),
-            pl.BlockSpec((1, padded, chans), lambda r: (r, 0, 0)),
+            pl.BlockSpec((1, width, chans), lambda r: (r, 0, 0)),
         ],
         out_specs=pl.BlockSpec((3 * chans, chans), lambda r: (0, 0)),
         compiler_params=params,
         cost_estimate=cost,
         name="channel_grad",
     )(filtered, slope).reshape(3, chans, chans)
-    partial_grad = lax.psum_scatter(local_grad, "lat", scatter_dimension=1, tiled=True)
-    mixing_grad = lax.psum_scatter(partial_grad, "lon", scatter_dimension=2, tiled=True)
-
-    slope = slope[:, :width]
+    mixing_grad = scatter_sum(local_grad)
+
     pole_slope = jnp.where(south, slope[:1], slope[-1:])
     pole_cycle = lax.all_gather(pole_slope, "lon", axis=1, tiled=True)
     slope_wide = widen(slope, padded)
     bwd_extra = polar_terms(
-        pole_cycle, flag, (lon_start - o_two[::1]) % cycle, jnp.transpose(w_two, (1, 0, 2)),
+        pole_cycle, flag, (lon_start - o_two) % cycle, jnp.transpose(w_two, (1, 0, 2)),
         [(0, 0), (1, 0)], 2, padded,
     )
     first = jnp.where(south, 0, rows - 2)
@@ -280,25 +301,38 @@
         flag[0] * ((row_ids >= first) & (row_ids < first + 2)) > 0, row_ids - first, -1
     ).astype(jnp.int32)
     bwd_base = base_rows(psi_loc, off_loc, polar_pad, rows, True)
-    state_grad = pl.pallas_call(
-        functools.partial(backward_kernel, blocks),
-        out_shape=jax.ShapeDtypeStruct(state.shape, BF16),
-        grid_spec=pltpu.PrefetchScalarGridSpec(
-            num_scalar_prefetch=1,
-            grid=(rows,),
-            in_specs=conv_specs(wl, padded, chans) + [field],
-            out_specs=field,
-            scratch_shapes=[
-                pltpu.VMEM((3 * TJ, SPAN), BF16),
-                pltpu.VMEM((SPAN, chans), BF16),
-                pltpu.VMEM((padded, 3 * chans), BF16),
-            ],
-        ),
-        compiler_params=params,
-        cost_estimate=cost,
-        name="backward",
-    )(bwd_slot, bwd_base, slope_wide, slope_wide, slope_wide, bwd_extra,
-      jnp.swapaxes(mixing, 1, 2).reshape(3 * chans, chans), cotangent)
+    mix_t = jnp.swapaxes(mixing, 1, 2).reshape(3 * chans, chans)
+    pieces = 3 if rows % 3 == 0 else 1
+    part = rows // pieces
+    state_grad = None
+    for piece in range(pieces):
+        at = piece * part
+        moved = pl.BlockSpec((1, width, chans), lambda r, slot, at=at: (r + at, 0, 0))
+        held = [] if state_grad is None else [state_grad]
+        state_grad = pl.pallas_call(
+            functools.partial(backward_kernel, blocks, at),
+            out_shape=jax.ShapeDtypeStruct(state.shape, BF16),
+            grid_spec=pltpu.PrefetchScalarGridSpec(
+                num_scalar_prefetch=1,
+                grid=(part,),
+                in_specs=conv_specs(wl, padded, chans, at) + [moved]
+                + [pl.BlockSpec(memory_space=pl.ANY)] * len(held),
+                out_specs=moved,
+                scratch_shapes=[
+                    pltpu.VMEM((3 * TJ, SPAN), BF16),
+                    pltpu.VMEM((SPAN, chans), BF16),
+                    pltpu.VMEM((padded, 3 * chans), BF16),
+                ],
+            ),
+            input_output_aliases={8: 0} if held else {},
+            compiler_params=params,
+            cost_estimate=pl.CostEstimate(
+                flops=flops // pieces,
+                bytes_accessed=rows * padded * chans * 20 // pieces,
+                transcendentals=0,
+            ),
+            name="backward_%d" % piece,
+        )(bwd_slot, bwd_base, slope_wide, slope_wide, slope_wide, bwd_extra, mix_t, cotangent, *held)
     return (output, mixing_grad, state_grad)
 
 

time: 228 us -> 195 us (0.86)
  waiting for transfers between devices: 103 us -> 35.2 us
  local copies, waits for them, and re-layouts: 18.6 us -> 37.7 us
  Pallas kernels: 63.8 us -> 71.3 us
  other arithmetic: 13.8 us -> 20.3 us
    reduce_scatter x2 -> x0, waiting for transfers between devices: 57.6 us -> none  [the longest x1 57.6 us: per_device(): lax.psum_scatter(local_grad, 'lat', scatter_dimension=1, tiled=True)]
    all_gather x1, waiting for transfers between devices: 16.5 us -> 0.01 us  [per_device(): pole_cycle = lax.all_gather(pole_slope, 'lon', axis=1, tiled=True)]
    ppermute x0 -> x5, waiting for transfers between devices: none -> 13.8 us  [scatter_sum(): got = lax.ppermute(theirs, axis, [(i, i ^ step) for i in range(count)])]
    ppermute x2, waiting for transfers between devices: 9.74 us -> 0.01 us  [widen(): after = lax.ppermute(shard[:1], 'lat', down)]
    dynamic_slice x0 -> x1, local copies, waits for them, and re-layouts: none -> 7.33 us  [scatter_sum(): mine = lax.dynamic_index_in_dim(halves, bit, 1, keepdims=False)]
    pallas_call x1 -> x3, Pallas kernels: 15.8 us -> 22.4 us  [per_device(): pl.pallas_call(functools.partial(backward_kernel, blocks, at), out_shape=...]
    ppermute x2, waiting for transfers between devices: 6.68 us -> 12.8 us  [widen(): before = lax.ppermute(shard[-1:], 'lat', up)]
    another operation x2 -> x3, local copies, waits for them, and re-layouts: 0.01 us -> 4.88 us  [the longest x1 4.88 us: scatter_sum(): left = local.reshape(k, nlat, chans // nlat, nlon, chans // nlon)]
  transfers between devices with their start and end apart: 12 -> 15, of which waited for: 8 -> 6; matrix products, arithmetic and copies ran while one was open for 11% -> 18% of each run, Pallas kernels for 11% -> 17%
where the time goes in v2:
time: 195 us; the launch traced here: 194 us
  Pallas kernels  71.3 us (37%)
  local copies, waits for them, and re-layouts  37.7 us (19%)
  waiting for transfers between devices  35.2 us (18%)
  other arithmetic  20.3 us (10%)
  between operations  14.8 us (8%)
  starting transfers between devices  14.6 us (7%)
    pallas_call x3, Pallas kernels, per_device(): pl.pallas_call(functools.partial(backward_kernel, blocks, at), out_shape=...  22.4 us
    pallas_call x2, Pallas kernels, polar_terms(): pl.pallas_call(functools.partial(polar_kernel, pairs, ntgt, cycle, padded...  19.6 us
    pallas_call x1, Pallas kernels, per_device(): pl.pallas_call(functools.partial(forward_kernel, blocks), out_shape=(jax....  17.4 us
    ppermute x5, waiting for transfers between devices, scatter_sum(): got = lax.ppermute(theirs, axis, [(i, i ^ step) for i in range(count)])  13.8 us
    ppermute x2, waiting for transfers between devices, widen(): before = lax.ppermute(shard[-1:], 'lat', up)  12.8 us
    pallas_call x1, Pallas kernels, per_device(): pl.pallas_call(functools.partial(grad_kernel, 1.0 / math.sqrt(nrings * cy...  12 us
    unnamed x45, local copies, waits for them, and re-layouts  9.07 us
    ppermute x2, starting transfers between devices, widen(): before = lax.ppermute(shard[-1:], 'lat', up)  7.91 us
  transfers between devices with their start and end apart: 15, of which 6 were waited for; matrix products, arithmetic and copies ran while one was open for 18% of the time, Pallas kernels for 17%

profile of v2, /device:TPU:0, one launch (start us, length us, event | category | flops | bytes accessed | tf_op | source)
XLA Modules:
  0.0 193.8 jit_solution(2274437598454121716)
XLA Ops:
  7.3 1.9 fusion.14
  9.2 5.8 %collective-permute-start = (bf16[1,360,512]{2,1,0:T(8,128)(2,1)}, bf16[1,360,512]{2,1,0:T(8,128)(2,1)}, u32[]{:S(2)}, u32[]{:S(2)}) collective-permute-start(bf16[1,360,512]{2,1,0:T(8,128)(2,1)} %get-tuple-element.23), channel_id=1, source_target_pairs={{0,4},{4,8},{8,12},{12,16},{16,20},{20,24},{24,28},{1,5},{5,9},{9,... | collective-permute-start | bytes 1105928 | tf_op jit(solution)/shard_map/ppermute | solution.py:26
  14.9 1.3 collective-permute-start.1
  16.2 2.3 %slice_select_fusion = bf16[2,360,512]{2,1,0:T(8,128)(2,1)} fusion(bf16[6,360,512]{2,1,0:T(8,128)(2,1)} %state_ref.1, pred[]{:T(512)S(6)} %eq.123), kind=kLoop, calls=%fused_computation.20 | loop fusion | flops 368640 | bytes 2211841 | tf_op jit(solution)/shard_map/jit(_where)/select_n | solution.py:241
  27.9 1.4 gather_fusion.7
  30.7 1.4 gather_fusion.10
  36.6 1.6 copy-done.8
  39.3 6.3 %collective-permute-done.3 = bf16[8,16,512]{2,1,0:T(8,128)(2,1)S(1)} collective-permute-done((bf16[8,16,512]{2,1,0:T(8,128)(2,1)S(1)}, bf16[8,16,512]{2,1,0:T(8,128)(2,1)S(1)}, u32[]{:S(2)}, u32[]{:S(2)}) %collective-permute-start.3) | collective-permute-done | bytes 131104 | tf_op jit(solution)/shard_map/ppermute | solution.py:32
  45.5 1.8 collective-permute-done.2
  47.3 4.4 %maximum_maximum_fusion.s0.s1.s2 = bf16[8,416,512]{2,1,0:T(8,128)(2,1)} fusion(bf16[8,16,512]{2,1,0:T(8,128)(2,1)S(1)} %collective-permute-done.3, bf16[8,360,512]{2,1,0:T(8,128)(2,1)} %copy-done.8, bf16[8,16,512]{2,1,0:T(8,128)(2,1)S(1)} %collective-permute-done.2, bf16[416]{0:T(512)(128)(2,1)S(1)} %pad.38.clone), kind=kLoop, calls=%fused_computation.13 | loop fusion | flops 13631488 | bytes 6619968 | tf_op jit(solution)/shard_map/concatenate | solution.py:37
  51.7 9.7 %polar.2.extra_ref = f32[3,384,512]{2,1,0:T(8,128)S(1)} custom-call(s32[1]{0:T(128)} %bitcast.4.flag_ref, s32[16]{0:T(128)S(1)} %reshape.144.start_ref, f32[48]{0:T(128)S(1)} %reshape.145.w_ref, bf16[2,1440,512]{2,1,0:T(8,128)(2,1)} %all-gather.3.cloned.1.call-done.g_ref), custom_call_target="tpu_custom_call" | custom-call | tf_op jit(solution)/shard_map/polar/pallas_call | solution.py:126
  61.5 1.5 copy-done.3
  62.9 17.4 %forward.1 = (bf16[6,360,512]{2,1,0:T(8,128)(2,1)}, bf16[6,360,512]{2,1,0:T(8,128)(2,1)S(1)}, bf16[6,384,1536]{2,1,0:T(8,128)(2,1)}) custom-call(s32[6]{0:T(128)S(1)} %or_select_fusion.slot_ref, f32[6,8,512]{2,1,0:T(8,128)S(1)} %pad.29.base_ref, bf16[8,416,512]{2,1,0:T(8,128)(2,1)} %maximum_maximum_fusion.s0.s1.s2, ...), custom_call_target="tpu_custom_call" | custom-call | flops 7247757312 | bytes 23592960 | tf_op jit(solution)/shard_map/forward/pallas_call | solution.py:254
  80.3 12.0 %channel_grad.1 = f32[1536,512]{1,0:T(8,128)} custom-call(bf16[6,384,1536]{2,1,0:T(8,128)(2,1)} %get-tuple-element.7.filt_ref, bf16[6,360,512]{2,1,0:T(8,128)(2,1)S(1)} %get-tuple-element.8.slope_ref), custom_call_target="tpu_custom_call" | custom-call | flops 7247757312 | bytes 23592960 | tf_op jit(solution)/shard_map/channel_grad/pallas_call | solution.py:277
  92.3 4.9 %reshape_reshape.3 = f32[3,8,64,4,128]{4,3,2,1,0:T(4,128)} reshape(f32[1536,512]{1,0:T(8,128)} %channel_grad.1) | data formatting | bytes 6291456 | tf_op jit(solution)/shard_map/reshape;reshape | solution.py:43
  97.2 7.3 %constant_dynamic-slice_fusion.1 = (f32[2,1,8,3,64,128]{5,1,0,4,2,3:T(1,128)}, f32[2,1,8,3,64,128]{5,1,0,4,2,3:T(1,128)S(1)}) fusion(f32[2,2,8,3,64,128]{5,1,0,4,2,3:T(2,128)} %bitcast.52, s32[]{:T(128)S(6)} %select_n.227, s32[]{:T(128)S(6)} %select_n.228), kind=kLoop, calls=%fused_computation.79 | loop fusion | bytes 6291464 | tf_op jit(solution)/shard_map/jit(dynamic_index_in_dim)/dynamic_slice | solution.py:56
  104.5 1.4 copy.113
  106.9 1.1 broadcast_select_fusion
  108.0 2.2 %collective-permute-start.9 = (bf16[1,360,512]{2,1,0:T(8,128)(2,1)}, bf16[1,360,512]{2,1,0:T(8,128)(2,1)}, u32[]{:S(2)}, u32[]{:S(2)}) collective-permute-start(bf16[1,360,512]{2,1,0:T(8,128)(2,1)} %get-tuple-element.21), channel_id=1, source_target_pairs={{0,4},{4,8},{8,12},{12,16},{16,20},{20,24},{24,28},{1,5},{5,9},{9,... | collective-permute-start | bytes 1105928 | tf_op jit(solution)/shard_map/ppermute | solution.py:26
  110.4 1.7 copy.97
  112.2 1.3 collective-permute-start.10
  113.5 12.8 %collective-permute-done.9 = bf16[1,360,512]{2,1,0:T(8,128)(2,1)} collective-permute-done((bf16[1,360,512]{2,1,0:T(8,128)(2,1)}, bf16[1,360,512]{2,1,0:T(8,128)(2,1)}, u32[]{:S(2)}, u32[]{:S(2)}) %collective-permute-start.9) | collective-permute-done | bytes 368672 | tf_op jit(solution)/shard_map/ppermute | solution.py:26
  127.4 1.6 fusion
  131.9 12.4 %collective-permute-done.5 = bf16[1,8,3,64,128]{4,3,2,1,0:T(8,128)(2,1)S(1)} collective-permute-done((bf16[1,8,3,64,128]{4,3,2,1,0:T(8,128)(2,1)S(1)}, bf16[1,8,3,64,128]{4,3,2,1,0:T(8,128)(2,1)S(1)}, u32[]{:S(2)}, u32[]{:S(2)}) %collective-permute-start.5) | collective-permute-done | bytes 393248 | tf_op jit(solution)/shard_map/ppermute | solution.py:60
  144.5 1.5 collective-permute-start.6
  146.5 3.0 %maximum_maximum_fusion.1.s0.s1.s2 = bf16[8,416,512]{2,1,0:T(8,128)(2,1)} fusion(bf16[8,16,512]{2,1,0:T(8,128)(2,1)S(1)} %collective-permute-done.12, bf16[8,360,512]{2,1,0:T(8,128)(2,1)S(1)} %constant_dynamic-update-slice_fusion.3, bf16[8,16,512]{2,1,0:T(8,128)(2,1)S(1)} %collective-permute-done.11, bf16[416]{0:T(512)(128)(2,1)S(1)} %pad.38.clone), kind=kLoop, calls=%fused_computation.14 | loop fusion | flops 13631488 | bytes 6619968 | tf_op jit(solution)/shard_map/concatenate | solution.py:37
  149.4 1.4 collective-permute-done.6
  151.6 1.4 copy-done.5
  153.0 9.9 %polar.3.extra_ref = f32[6,384,512]{2,1,0:T(8,128)} custom-call(s32[1]{0:T(128)} %bitcast.4.flag_ref, s32[16]{0:T(128)S(1)} %reshape.149.start_ref, f32[48]{0:T(128)S(1)} %reshape.145.w_ref, bf16[1,1440,512]{2,1,0:T(8,128)(2,1)S(1)} %copy-done.5), custom_call_target="tpu_custom_call" | custom-call | tf_op jit(solution)/shard_map/polar/pallas_call | solution.py:126
  162.8 7.7 %backward_0.1.rest_0_ = bf16[6,360,512]{2,1,0:T(8,128)(2,1)} custom-call(s32[6]{0:T(128)S(1)} %compare_select_fusion.slot_ref, f32[6,8,512]{2,1,0:T(8,128)S(1)} %pad.30.base_ref, bf16[8,416,512]{2,1,0:T(8,128)(2,1)} %maximum_maximum_fusion.1.s0.s1.s2, bf16[8,416,512]{2,1,0:T(8,128)(2,1)} %maximum_maximum_fusion.1.s0.s1.s2, ...), custom_call_target="tpu_custom_call" | custom-call | flops 2415919104 | bytes 7864320 | tf_op jit(solution)/shard_map/backward_0/pallas_call | solution.py:312
  170.6 7.3 %backward_1.1.rest_0_ = bf16[6,360,512]{2,1,0:T(8,128)(2,1)} custom-call(s32[6]{0:T(128)S(1)} %compare_select_fusion.slot_ref, f32[6,8,512]{2,1,0:T(8,128)S(1)} %pad.30.base_ref, bf16[8,416,512]{2,1,0:T(8,128)(2,1)} %maximum_maximum_fusion.1.s0.s1.s2, bf16[8,416,512]{2,1,0:T(8,128)(2,1)} %maximum_maximum_fusion.1.s0.s1.s2, ...), custom_call_target="tpu_custom_call", output_to_operand_aliasing={{}: (8, {})} | custom-call | flops 2415919104 | bytes 7864320 | tf_op jit(solution)/shard_map/backward_1/pallas_call | solution.py:312
  179.0 7.4 %backward_2.1 = bf16[6,360,512]{2,1,0:T(8,128)(2,1)} custom-call(s32[6]{0:T(128)S(1)} %compare_select_fusion.slot_ref, f32[6,8,512]{2,1,0:T(8,128)S(1)} %pad.30.base_ref, bf16[8,416,512]{2,1,0:T(8,128)(2,1)} %maximum_maximum_fusion.1.s0.s1.s2, bf16[8,416,512]{2,1,0:T(8,128)(2,1)} %maximum_maximum_fusion.1.s0.s1.s2, ...), custom_call_target="tpu_custom_call", output_to_operand_aliasing={{}: (8, {})} | custom-call | flops 2415919104 | bytes 7864320 | tf_op jit(solution)/shard_map/backward_2/pallas_call | solution.py:312
  (140 shorter events, 24.2 us)
Async XLA Ops:
  7.2 11.8 %copy-start.13 = (s32[6]{0:T(128)S(1)}, s32[6]{0:T(128)}, u32[]{:S(2)}) copy-start(s32[6]{0:T(128)} %constant.364) | copy-start | bytes 76
  7.2 12.4 %copy-start.16 = (s32[6]{0:T(128)S(1)}, s32[6]{0:T(128)}, u32[]{:S(2)}) copy-start(s32[6]{0:T(128)} %constant.381) | copy-start | bytes 76
  7.2 14.8 %copy-start.15 = (s32[6]{0:T(128)S(1)}, s32[6]{0:T(128)}, u32[]{:S(2)}) copy-start(s32[6]{0:T(128)} %constant.397) | copy-start | bytes 76
  7.2 18.3 %copy-start.12 = (s32[6]{0:T(128)S(1)}, s32[6]{0:T(128)}, u32[]{:S(2)}) copy-start(s32[6]{0:T(128)} %constant.413) | copy-start | bytes 76
  7.2 11.4 %copy-start.18 = (s32[48,3,8]{0,2,1:T(8,128)S(1)}, s32[48,3,8]{0,2,1:T(8,128)}, u32[]{:S(2)}) copy-start(s32[48,3,8]{0,2,1:T(8,128)} %param.31) | copy-start | bytes 13828
  7.2 11.5 %copy-start.17 = (f32[3,48,3,8]{1,3,2,0:T(8,128)S(1)}, f32[3,48,3,8]{1,3,2,0:T(8,128)}, u32[]{:S(2)}) copy-start(f32[3,48,3,8]{1,3,2,0:T(8,128)} %param.30) | copy-start | bytes 41476
  7.2 44.5 %all-gather.3.cloned.1.call-start = ((), (), s32[]{:S(2)}) async-start(), calls=%async_computation | async-start | bytes 3686400 | tf_op jit(solution)/shard_map/all_gather | solution.py:242
  9.2 21.6 %copy-start.14 = (s32[6]{0:T(128)S(1)}, s32[6]{0:T(128)}, u32[]{:S(2)}) copy-start(s32[6]{0:T(128)} %constant.430) | copy-start | bytes 76
  9.2 26.2 %collective-permute-start = (bf16[1,360,512]{2,1,0:T(8,128)(2,1)}, bf16[1,360,512]{2,1,0:T(8,128)(2,1)}, u32[]{:S(2)}, u32[]{:S(2)}) collective-permute-start(bf16[1,360,512]{2,1,0:T(8,128)(2,1)} %get-tuple-element.23), channel_id=1, source_target_pairs={{0,4},{4,8},{8,12},{12,16},{16,20},{20,24},{24,28},{1,5},{5,9},{9,... | collective-permute-start | bytes 1105928 | tf_op jit(solution)/shard_map/ppermute | solution.py:26
  14.9 21.6 %collective-permute-start.1 = (bf16[1,360,512]{2,1,0:T(8,128)(2,1)S(1)}, bf16[1,360,512]{2,1,0:T(8,128)(2,1)S(1)}, u32[]{:S(2)}, u32[]{:S(2)}) collective-permute-start(bf16[1,360,512]{2,1,0:T(8,128)(2,1)S(1)} %get-tuple-element.22), channel_id=1, source_target_pairs={{4,0},{8,4},{12,8},{16,12},{20,16},{24,20},{28,24},{5,1},{9,5},{13... | collective-permute-start | bytes 1105928 | tf_op jit(solution)/shard_map/ppermute | solution.py:27
  18.5 17.9 %copy-start.6 = (bf16[6,360,512]{2,1,0:T(8,128)(2,1)S(1)}, bf16[6,360,512]{2,1,0:T(8,128)(2,1)}, u32[]{:S(2)}) copy-start(bf16[6,360,512]{2,1,0:T(8,128)(2,1)} %state_ref.1) | copy-start | bytes 6635524
  18.5 133.1 %all-gather.5.cloned.1.call-start = ((), (), s32[]{:S(2)}) async-start(), calls=%async_computation.1 | async-start | bytes 1843200 | tf_op jit(solution)/shard_map/all_gather | solution.py:293
  19.0 3.7 %copy-start.11 = (f32[3,8,3,8]{3,0,2,1:T(4,128)}, f32[3,8,3,8]{3,0,2,1:T(4,128)S(1)}, u32[]{:S(2)}) copy-start(f32[3,8,3,8]{3,0,2,1:T(4,128)S(1)} %pad_dynamic-slice_fusion.2) | copy-start | bytes 6916
  36.6 1.6 copy-start.8
  38.3 7.3 %collective-permute-start.3 = (bf16[8,16,512]{2,1,0:T(8,128)(2,1)S(1)}, bf16[8,16,512]{2,1,0:T(8,128)(2,1)S(1)}, u32[]{:S(2)}, u32[]{:S(2)}) collective-permute-start(bf16[8,16,512]{2,1,0:T(8,128)(2,1)S(1)} %get-tuple-element.18), channel_id=1, source_target_pairs={{1,0},{2,1},{3,2},{0,3},{5,4},{6,5},{7,6},{4,7},{9,8},{10,9},{11,1... | collective-permute-start | bytes 393224 | tf_op jit(solution)/shard_map/ppermute | solution.py:32
  39.0 8.4 %collective-permute-start.2 = (bf16[8,16,512]{2,1,0:T(8,128)(2,1)S(1)}, bf16[8,16,512]{2,1,0:T(8,128)(2,1)S(1)}, u32[]{:S(2)}, u32[]{:S(2)}) collective-permute-start(bf16[8,16,512]{2,1,0:T(8,128)(2,1)S(1)} %get-tuple-element.17), channel_id=1, source_target_pairs={{0,1},{1,2},{2,3},{3,0},{4,5},{5,6},{6,7},{7,4},{8,9},{9,10},{10,1... | collective-permute-start | bytes 393224 | tf_op jit(solution)/shard_map/ppermute | solution.py:31
  51.7 11.2 %copy-start.4 = (bf16[3,512,512]{2,1,0:T(8,128)(2,1)S(1)}, bf16[3,512,512]{2,1,0:T(8,128)(2,1)}, u32[]{:S(2)}) copy-start(bf16[3,512,512]{2,1,0:T(8,128)(2,1)} %param.32) | copy-start | bytes 4718596
  61.5 1.5 copy-start.3
  80.3 26.6 %copy-start.1 = (bf16[6,360,512]{2,1,0:T(8,128)(2,1)}, bf16[6,360,512]{2,1,0:T(8,128)(2,1)S(1)}, u32[]{:S(2)}) copy-start(bf16[6,360,512]{2,1,0:T(8,128)(2,1)S(1)} %get-tuple-element.8.slope_ref) | copy-start | bytes 6635524
  105.9 21.5 %collective-permute-start.4 = (f32[2,8,3,64,128]{4,3,2,1,0:T(8,128)}, f32[2,8,3,64,128]{4,3,2,1,0:T(8,128)}, u32[]{:S(2)}, u32[]{:S(2)}) collective-permute-start(f32[2,8,3,64,128]{4,3,2,1,0:T(8,128)} %bitcast.45), channel_id=1, source_target_pairs={{0,1},{1,0},{2,3},{3,2},{4,5},{5,4},{6,7},{7,6},{8,9},{9,8},{10,11... | collective-permute-start | bytes 4718600 | tf_op jit(solution)/shard_map/ppermute | solution.py:60
  108.0 19.4 %copy-start.7 = (f32[2,1,8,3,64,128]{5,1,0,4,2,3:T(1,128)S(1)}, f32[2,1,8,3,64,128]{5,1,0,4,2,3:T(1,128)}, u32[]{:S(2)}) copy-start(f32[2,1,8,3,64,128]{5,1,0,4,2,3:T(1,128)} %get-tuple-element.13) | copy-start | bytes 4718596
  108.0 18.4 %collective-permute-start.9 = (bf16[1,360,512]{2,1,0:T(8,128)(2,1)}, bf16[1,360,512]{2,1,0:T(8,128)(2,1)}, u32[]{:S(2)}, u32[]{:S(2)}) collective-permute-start(bf16[1,360,512]{2,1,0:T(8,128)(2,1)} %get-tuple-element.21), channel_id=1, source_target_pairs={{0,4},{4,8},{8,12},{12,16},{16,20},{20,24},{24,28},{1,5},{5,9},{9,... | collective-permute-start | bytes 1105928 | tf_op jit(solution)/shard_map/ppermute | solution.py:26
  112.2 18.1 %collective-permute-start.10 = (bf16[1,360,512]{2,1,0:T(8,128)(2,1)}, bf16[1,360,512]{2,1,0:T(8,128)(2,1)}, u32[]{:S(2)}, u32[]{:S(2)}) collective-permute-start(bf16[1,360,512]{2,1,0:T(8,128)(2,1)} %get-tuple-element.20), channel_id=1, source_target_pairs={{4,0},{8,4},{12,8},{16,12},{20,16},{24,20},{28,24},{5,1},{9,5},{13... | collective-permute-start | bytes 1105928 | tf_op jit(solution)/shard_map/ppermute | solution.py:27
  113.5 16.7 %copy-start.2 = (bf16[6,360,512]{2,1,0:T(8,128)(2,1)S(1)}, bf16[6,360,512]{2,1,0:T(8,128)(2,1)}, u32[]{:S(2)}) copy-start(bf16[6,360,512]{2,1,0:T(8,128)(2,1)} %copy-done.1) | copy-start | bytes 6635524
  129.1 15.2 %collective-permute-start.5 = (bf16[1,8,3,64,128]{4,3,2,1,0:T(8,128)(2,1)S(1)}, bf16[1,8,3,64,128]{4,3,2,1,0:T(8,128)(2,1)S(1)}, u32[]{:S(2)}, u32[]{:S(2)}) collective-permute-start(bf16[1,8,3,64,128]{4,3,2,1,0:T(8,128)(2,1)S(1)} %dynamic-slice_convert_fusion), channel_id=1, source_target_pairs={{0,2},{1,3},{2,0},{3,1},{4,6},{5,7},{6,4},{7,5},{8,10},{9,11},{10,... | collective-permute-start | bytes 1179656 | tf_op jit(solution)/shard_map/ppermute | solution.py:60
  131.4 14.7 %collective-permute-start.12 = (bf16[8,16,512]{2,1,0:T(8,128)(2,1)S(1)}, bf16[8,16,512]{2,1,0:T(8,128)(2,1)S(1)}, u32[]{:S(2)}, u32[]{:S(2)}) collective-permute-start(bf16[8,16,512]{2,1,0:T(8,128)(2,1)S(1)} %get-tuple-element.16), channel_id=1, source_target_pairs={{1,0},{2,1},{3,2},{0,3},{5,4},{6,5},{7,6},{4,7},{9,8},{10,9},{11,1... | collective-permute-start | bytes 393224 | tf_op jit(solution)/shard_map/ppermute | solution.py:32
  131.7 14.7 %collective-permute-start.11 = (bf16[8,16,512]{2,1,0:T(8,128)(2,1)S(1)}, bf16[8,16,512]{2,1,0:T(8,128)(2,1)S(1)}, u32[]{:S(2)}, u32[]{:S(2)}) collective-permute-start(bf16[8,16,512]{2,1,0:T(8,128)(2,1)S(1)} %get-tuple-element.15), channel_id=1, source_target_pairs={{0,1},{1,2},{2,3},{3,0},{4,5},{5,6},{6,7},{7,4},{8,9},{9,10},{10,1... | collective-permute-start | bytes 393224 | tf_op jit(solution)/shard_map/ppermute | solution.py:31
  144.5 6.3 %collective-permute-start.6 = (bf16[4,3,64,128]{3,2,1,0:T(8,128)(2,1)S(1)}, bf16[4,3,64,128]{3,2,1,0:T(8,128)(2,1)S(1)}, u32[]{:S(2)}, u32[]{:S(2)}) collective-permute-start(bf16[4,3,64,128]{3,2,1,0:T(8,128)(2,1)S(1)} %fusion.1), channel_id=1, source_target_pairs={{0,4},{4,0},{8,12},{12,8},{16,20},{20,16},{24,28},{28,24},{1,5},{5... | collective-permute-start | bytes 589832 | tf_op jit(solution)/shard_map/ppermute | solution.py:60
  150.9 27.0 %collective-permute-start.7 = (f32[2,3,64,128]{3,2,1,0:T(8,128)S(1)}, f32[2,3,64,128]{3,2,1,0:T(8,128)}, u32[]{:S(2)}, u32[]{:S(2)}) collective-permute-start(f32[2,3,64,128]{3,2,1,0:T(8,128)S(1)} %dynamic-slice_bitcast_fusion), channel_id=1, source_target_pairs={{0,8},{4,12},{8,0},{12,4},{16,24},{20,28},{24,16},{28,20},{1,9},{5... | collective-permute-start | bytes 589832 | tf_op jit(solution)/shard_map/ppermute | solution.py:60
  153.0 9.9 %copy-start = (bf16[6,360,512]{2,1,0:T(8,128)(2,1)S(1)}, bf16[6,360,512]{2,1,0:T(8,128)(2,1)}, u32[]{:S(2)}) copy-start(bf16[6,360,512]{2,1,0:T(8,128)(2,1)} %cot_ref.7) | copy-start | bytes 6635524
  170.6 7.3 %copy-start.10 = (f32[4,3,64,128]{3,2,1,0:T(8,128)S(1)}, f32[4,3,64,128]{3,2,1,0:T(8,128)}, u32[]{:S(2)}) copy-start(f32[4,3,64,128]{3,2,1,0:T(8,128)} %copy-done.9) | copy-start | bytes 1179652
  178.9 7.4 %collective-permute-start.8 = (f32[1,3,64,128]{3,2,1,0:T(8,128)S(1)}, f32[1,3,64,128]{3,2,1,0:T(8,128)S(1)}, u32[]{:S(2)}, u32[]{:S(2)}) collective-permute-start(f32[1,3,64,128]{3,2,1,0:T(8,128)S(1)} %constant_dynamic-slice_fusion.2), channel_id=1, source_target_pairs={{0,16},{4,20},{8,24},{12,28},{16,0},{20,4},{24,8},{28,12},{1,17},{... | collective-permute-start | bytes 294920 | tf_op jit(solution)/shard_map/ppermute | solution.py:60
  (2 other events, 2.1 us)
Sparse Core Ops, SparseCore 0:
  18.6 31.8 all-gather.2
  113.6 27.1 all-gather.4

commit v3 on v2

--- a/solution.py
+++ b/solution.py
@@ -37,11 +37,7 @@
     return jnp.concatenate(parts, axis=1)
 
 
-def scatter_sum(local):
-    k, chans, _ = local.shape
-    nlat, nlon = lax.axis_size("lat"), lax.axis_size("lon")
-    left = local.reshape(k, nlat, chans // nlat, nlon, chans // nlon)
-    left = jnp.transpose(left, (3, 1, 0, 2, 4))
+def scatter_sum(left):
     for dim, axis in enumerate(("lon", "lat")):
         count = lax.axis_size(axis)
         index = lax.axis_index(axis)
@@ -181,23 +177,32 @@
     grad_ref[0] = (cot_ref[0].astype(F32) + back).astype(BF16)
 
 
-def grad_kernel(scale, filt_ref, slope_ref, out_ref):
+def grad_kernel(scale, filt_ref, slope_ref, out_ref, total):
     r = pl.program_id(0)
     term = lax.dot_general(
-        filt_ref[0, : slope_ref.shape[1], :], slope_ref[0], (((0,), (0,)), ((), ())), preferred_element_type=F32
+        filt_ref[0, : slope_ref.shape[1], :], slope_ref[0], (((0,), (0,)), ((), ())),
+        preferred_element_type=F32,
     )
 
     @pl.when(r == 0)
     def _():
-        out_ref[...] = term
+        total[...] = term
 
     @pl.when(r > 0)
     def _():
-        out_ref[...] += term
+        total[...] += term
 
     @pl.when(r == pl.num_programs(0) - 1)
     def _():
-        out_ref[...] *= scale
+        if len(out_ref.shape) == 2:
+            out_ref[...] = total[...] * scale
+            return
+        nlon, nlat, _, cr, cc = out_ref.shape
+        for q in range(nlon):
+            for b in range(nlat):
+                for k in range(3):
+                    at = (k * nlat + b) * cr
+                    out_ref[q, b, k] = total[at : at + cr, q * cc : (q + 1) * cc] * scale
 
 
 def conv_specs(wl, padded, chans, at=0):
@@ -274,19 +279,26 @@
         name="forward",
     )(fwd_slot, fwd_base, wide, wide, wide, fwd_extra, mixing.reshape(3 * chans, chans), state, cotangent)
 
+    cr, cc = chans // nlat, chans // nlon
+    direct = cr % 8 == 0 and cc % 128 == 0
+    grad_shape = (nlon, nlat, 3, cr, cc) if direct else (3 * chans, chans)
     local_grad = pl.pallas_call(
         functools.partial(grad_kernel, 1.0 / math.sqrt(nrings * cycle)),
-        out_shape=jax.ShapeDtypeStruct((3 * chans, chans), F32),
+        out_shape=jax.ShapeDtypeStruct(grad_shape, F32),
         grid=(rows,),
         in_specs=[
             pl.BlockSpec((1, padded, 3 * chans), lambda r: (r, 0, 0)),
             pl.BlockSpec((1, width, chans), lambda r: (r, 0, 0)),
         ],
-        out_specs=pl.BlockSpec((3 * chans, chans), lambda r: (0, 0)),
+        out_specs=pl.BlockSpec(grad_shape, lambda r: (0,) * len(grad_shape)),
+        scratch_shapes=[pltpu.VMEM((3 * chans, chans), F32)],
         compiler_params=params,
         cost_estimate=cost,
         name="channel_grad",
-    )(filtered, slope).reshape(3, chans, chans)
+    )(filtered, slope)
+    if not direct:
+        local_grad = local_grad.reshape(3, nlat, cr, nlon, cc)
+        local_grad = jnp.transpose(local_grad, (3, 1, 0, 2, 4))
     mixing_grad = scatter_sum(local_grad)
 
     pole_slope = jnp.where(south, slope[:1], slope[-1:])

time: 195 us -> 178 us (0.913)
  local copies, waits for them, and re-layouts: 37.7 us -> 24.2 us
  waiting for transfers between devices: 35.2 us -> 32 us
    dynamic_slice x1 -> x0, local copies, waits for them, and re-layouts: 7.33 us -> none  [scatter_sum(): mine = lax.dynamic_index_in_dim(halves, bit, 1, keepdims=False)]
    another operation x3 -> x2, local copies, waits for them, and re-layouts: 4.88 us -> 0.01 us  [the longest x1 4.88 us: scatter_sum(): left = local.reshape(k, nlat, chans // nlat, nlon, chans // nlon)]
    unnamed x45 -> x38, local copies, waits for them, and re-layouts: 9.07 us -> 6.1 us
    ppermute x5, waiting for transfers between devices: 13.8 us -> 10.9 us  [scatter_sum(): got = lax.ppermute(theirs, axis, [(i, i ^ step) for i in range(count)])]
    squeeze x2 -> x3, local copies, waits for them, and re-layouts: 0.04 us -> 2.77 us  [scatter_sum(): theirs = lax.dynamic_index_in_dim(halves, 1 - bit, 1, keepdims=False)]
  transfers between devices with their start and end apart: 15 -> 15, of which waited for: 6 -> 5; matrix products, arithmetic and copies ran while one was open for 18% -> 19% of each run, Pallas kernels for 17% -> 18%
where the time goes in v3:
time: 178 us; the launch traced here: 177 us
  Pallas kernels  71.5 us (40%)
  waiting for transfers between devices  32 us (18%)
  local copies, waits for them, and re-layouts  24.2 us (14%)
  other arithmetic  19.6 us (11%)
  starting transfers between devices  14.8 us (8%)
  between operations  14.8 us (8%)
    pallas_call x3, Pallas kernels, per_device(): pl.pallas_call(functools.partial(backward_kernel, blocks, at), out_shape=...  22.4 us
    pallas_call x2, Pallas kernels, polar_terms(): pl.pallas_call(functools.partial(polar_kernel, pairs, ntgt, cycle, padded...  19.4 us
    pallas_call x1, Pallas kernels, per_device(): pl.pallas_call(functools.partial(forward_kernel, blocks), out_shape=(jax....  17.6 us
    ppermute x2, waiting for transfers between devices, widen(): before = lax.ppermute(shard[-1:], 'lat', up)  12.9 us
    pallas_call x1, Pallas kernels, per_device(): pl.pallas_call(functools.partial(grad_kernel, 1.0 / math.sqrt(nrings * cy...  12 us
    ppermute x5, waiting for transfers between devices, scatter_sum(): got = lax.ppermute(theirs, axis, [(i, i ^ step) for i in range(count)])  10.9 us
    concatenate x2, other arithmetic, widen(): return jnp.concatenate(parts, axis=1)  7.28 us
    ppermute x2, starting transfers between devices, widen(): before = lax.ppermute(shard[-1:], 'lat', up)  7.04 us
  transfers between devices with their start and end apart: 15, of which 5 were waited for; matrix products, arithmetic and copies ran while one was open for 19% of the time, Pallas kernels for 18%

profile of v3, /device:TPU:0, one launch (start us, length us, event | category | flops | bytes accessed | tf_op | source)
XLA Modules:
  0.0 176.9 jit_solution(11628795312658182773)
XLA Ops:
  7.3 1.9 %fusion.13 = (bf16[1,360,512]{2,1,0:T(8,128)(2,1)S(1)}, bf16[1,360,512]{2,1,0:T(8,128)(2,1)}) fusion(bf16[6,360,512]{2,1,0:T(8,128)(2,1)} %state_ref.1), kind=kLoop, calls=%fused_computation.95 | loop fusion | bytes 1474560 | tf_op jit(solution)/shard_map/slice | solution.py:27
  9.2 5.7 %collective-permute-start = (bf16[1,360,512]{2,1,0:T(8,128)(2,1)}, bf16[1,360,512]{2,1,0:T(8,128)(2,1)}, u32[]{:S(2)}, u32[]{:S(2)}) collective-permute-start(bf16[1,360,512]{2,1,0:T(8,128)(2,1)} %get-tuple-element.21), channel_id=1, source_target_pairs={{0,4},{4,8},{8,12},{12,16},{16,20},{20,24},{24,28},{1,5},{5,9},{9,... | collective-permute-start | bytes 1105928 | tf_op jit(solution)/shard_map/ppermute | solution.py:26
  14.9 1.3 collective-permute-start.1
  16.2 2.3 %slice_select_fusion = bf16[2,360,512]{2,1,0:T(8,128)(2,1)} fusion(bf16[6,360,512]{2,1,0:T(8,128)(2,1)} %state_ref.1, pred[]{:T(512)S(6)} %eq.123), kind=kLoop, calls=%fused_computation.19 | loop fusion | flops 368640 | bytes 2211841 | tf_op jit(solution)/shard_map/jit(_where)/select_n | solution.py:246
  27.9 1.4 gather_fusion.10
  29.3 1.4 gather_fusion.7
  33.9 0.8 add.259
  35.4 1.0 constant_dynamic-update-slice_fusion.2
  36.6 1.6 copy-done.7
  39.3 6.3 %collective-permute-done.3 = bf16[8,16,512]{2,1,0:T(8,128)(2,1)S(1)} collective-permute-done((bf16[8,16,512]{2,1,0:T(8,128)(2,1)S(1)}, bf16[8,16,512]{2,1,0:T(8,128)(2,1)S(1)}, u32[]{:S(2)}, u32[]{:S(2)}) %collective-permute-start.3) | collective-permute-done | bytes 131104 | tf_op jit(solution)/shard_map/ppermute | solution.py:32
  45.5 1.8 %collective-permute-done.2 = bf16[8,16,512]{2,1,0:T(8,128)(2,1)S(1)} collective-permute-done((bf16[8,16,512]{2,1,0:T(8,128)(2,1)S(1)}, bf16[8,16,512]{2,1,0:T(8,128)(2,1)S(1)}, u32[]{:S(2)}, u32[]{:S(2)}) %collective-permute-start.2) | collective-permute-done | bytes 131104 | tf_op jit(solution)/shard_map/ppermute | solution.py:31
  47.3 4.3 %maximum_maximum_fusion.s0.s1.s2 = bf16[8,416,512]{2,1,0:T(8,128)(2,1)} fusion(bf16[8,16,512]{2,1,0:T(8,128)(2,1)S(1)} %collective-permute-done.3, bf16[8,360,512]{2,1,0:T(8,128)(2,1)} %copy-done.7, bf16[8,16,512]{2,1,0:T(8,128)(2,1)S(1)} %collective-permute-done.2, bf16[416]{0:T(512)(128)(2,1)S(1)} %pad.38.clone), kind=kLoop, calls=%fused_computation.13 | loop fusion | flops 13631488 | bytes 6619968 | tf_op jit(solution)/shard_map/concatenate | solution.py:37
  51.7 9.6 %polar.2.extra_ref = f32[3,384,512]{2,1,0:T(8,128)S(1)} custom-call(s32[1]{0:T(128)} %bitcast.4.flag_ref, s32[16]{0:T(128)S(1)} %reshape.144.start_ref, f32[48]{0:T(128)S(1)} %reshape.145.w_ref, bf16[2,1440,512]{2,1,0:T(8,128)(2,1)} %all-gather.3.cloned.1.call-done.g_ref), custom_call_target="tpu_custom_call" | custom-call | tf_op jit(solution)/shard_map/polar/pallas_call | solution.py:122
  61.2 1.4 copy-done.3
  62.7 17.6 %forward.1 = (bf16[6,360,512]{2,1,0:T(8,128)(2,1)}, bf16[6,360,512]{2,1,0:T(8,128)(2,1)S(1)}, bf16[6,384,1536]{2,1,0:T(8,128)(2,1)}) custom-call(s32[6]{0:T(128)S(1)} %or_select_fusion.slot_ref, f32[6,8,512]{2,1,0:T(8,128)S(1)} %pad.29.base_ref, bf16[8,416,512]{2,1,0:T(8,128)(2,1)} %maximum_maximum_fusion.s0.s1.s2, ...), custom_call_target="tpu_custom_call" | custom-call | flops 7247757312 | bytes 23592960 | tf_op jit(solution)/shard_map/forward/pallas_call | solution.py:259
  80.3 12.0 %channel_grad.1 = f32[4,8,3,64,128]{4,3,2,1,0:T(8,128)} custom-call(bf16[6,384,1536]{2,1,0:T(8,128)(2,1)} %get-tuple-element.7.filt_ref, bf16[6,360,512]{2,1,0:T(8,128)(2,1)S(1)} %get-tuple-element.8.slope_ref), custom_call_target="tpu_custom_call" | custom-call | flops 7247757312 | bytes 23592960 | tf_op jit(solution)/shard_map/channel_grad/pallas_call | solution.py:285
  92.4 2.7 %dynamic-slice_bitcast_fusion = f32[2,8,3,64,128]{4,3,2,1,0:T(8,128)} fusion(f32[2,2,8,3,64,128]{5,4,3,2,1,0:T(8,128)} %bitcast.47, s32[]{:T(128)S(6)} %select_n.228), kind=kLoop, calls=%fused_computation.16 | loop fusion | bytes 3145732 | tf_op jit(solution)/shard_map/jit(dynamic_index_in_dim)/squeeze | solution.py:53
  96.0 0.8 broadcast_select_fusion
  96.8 1.3 collective-permute-start.9
  98.6 1.7 copy.91
  100.4 1.4 collective-permute-start.10
  101.8 12.9 %collective-permute-done.9 = bf16[1,360,512]{2,1,0:T(8,128)(2,1)S(1)} collective-permute-done((bf16[1,360,512]{2,1,0:T(8,128)(2,1)S(1)}, bf16[1,360,512]{2,1,0:T(8,128)(2,1)S(1)}, u32[]{:S(2)}, u32[]{:S(2)}) %collective-permute-start.9) | collective-permute-done | bytes 368672 | tf_op jit(solution)/shard_map/ppermute | solution.py:26
  114.8 2.2 %bitcast_add_fusion = f32[2,8,3,64,128]{4,3,2,1,0:T(8,128)S(1)} fusion(f32[2,8,3,64,128]{4,3,2,1,0:T(8,128)} %collective-permute-done.4, f32[2,2,8,3,64,128]{5,4,3,2,1,0:T(8,128)} %bitcast.48, s32[]{:T(128)S(6)} %select_n.227), kind=kLoop, calls=%fused_computation.15 | loop fusion | flops 393216 | bytes 4718596 | tf_op jit(solution)/shard_map/add | solution.py:57
  117.0 1.0 collective-permute-start.5
  118.9 10.2 %collective-permute-done.5 = bf16[1,8,3,64,128]{4,3,2,1,0:T(8,128)(2,1)S(1)} collective-permute-done((bf16[1,8,3,64,128]{4,3,2,1,0:T(8,128)(2,1)S(1)}, bf16[1,8,3,64,128]{4,3,2,1,0:T(8,128)(2,1)S(1)}, u32[]{:S(2)}, u32[]{:S(2)}) %collective-permute-start.5) | collective-permute-done | bytes 393248 | tf_op jit(solution)/shard_map/ppermute | solution.py:56
  129.3 2.5 %collective-permute-start.6 = (bf16[4,3,64,128]{3,2,1,0:T(8,128)(2,1)S(1)}, bf16[4,3,64,128]{3,2,1,0:T(8,128)(2,1)S(1)}, u32[]{:S(2)}, u32[]{:S(2)}) collective-permute-start(bf16[4,3,64,128]{3,2,1,0:T(8,128)(2,1)S(1)} %fusion), channel_id=1, source_target_pairs={{0,4},{4,0},{8,12},{12,8},{16,20},{20,16},{24,28},{28,24},{1,5},{5... | collective-permute-start | bytes 589832 | tf_op jit(solution)/shard_map/ppermute | solution.py:56
  131.8 2.9 %maximum_maximum_fusion.1.s0.s1.s2 = bf16[8,416,512]{2,1,0:T(8,128)(2,1)} fusion(bf16[8,16,512]{2,1,0:T(8,128)(2,1)S(1)} %collective-permute-done.12, bf16[8,360,512]{2,1,0:T(8,128)(2,1)S(1)} %constant_dynamic-update-slice_fusion.3, bf16[8,16,512]{2,1,0:T(8,128)(2,1)S(1)} %collective-permute-done.11, bf16[416]{0:T(512)(128)(2,1)S(1)} %pad.38.clone), kind=kLoop, calls=%fused_computation.14 | loop fusion | flops 13631488 | bytes 6619968 | tf_op jit(solution)/shard_map/concatenate | solution.py:37
  135.7 1.4 copy-done.5
  137.0 9.8 %polar.3.extra_ref = f32[6,384,512]{2,1,0:T(8,128)} custom-call(s32[1]{0:T(128)} %bitcast.4.flag_ref, s32[16]{0:T(128)S(1)} %reshape.149.start_ref, f32[48]{0:T(128)S(1)} %reshape.145.w_ref, bf16[1,1440,512]{2,1,0:T(8,128)(2,1)S(1)} %copy-done.5), custom_call_target="tpu_custom_call" | custom-call | tf_op jit(solution)/shard_map/polar/pallas_call | solution.py:122
  146.9 7.7 %backward_0.1.rest_0_ = bf16[6,360,512]{2,1,0:T(8,128)(2,1)} custom-call(s32[6]{0:T(128)S(1)} %compare_select_fusion.slot_ref, f32[6,8,512]{2,1,0:T(8,128)S(1)} %pad.30.base_ref, bf16[8,416,512]{2,1,0:T(8,128)(2,1)} %maximum_maximum_fusion.1.s0.s1.s2, bf16[8,416,512]{2,1,0:T(8,128)(2,1)} %maximum_maximum_fusion.1.s0.s1.s2, ...), custom_call_target="tpu_custom_call" | custom-call | flops 2415919104 | bytes 7864320 | tf_op jit(solution)/shard_map/backward_0/pallas_call | solution.py:324
  154.6 7.3 %backward_1.1.rest_0_ = bf16[6,360,512]{2,1,0:T(8,128)(2,1)} custom-call(s32[6]{0:T(128)S(1)} %compare_select_fusion.slot_ref, f32[6,8,512]{2,1,0:T(8,128)S(1)} %pad.30.base_ref, bf16[8,416,512]{2,1,0:T(8,128)(2,1)} %maximum_maximum_fusion.1.s0.s1.s2, bf16[8,416,512]{2,1,0:T(8,128)(2,1)} %maximum_maximum_fusion.1.s0.s1.s2, ...), custom_call_target="tpu_custom_call", output_to_operand_aliasing={{}: (8, {})} | custom-call | flops 2415919104 | bytes 7864320 | tf_op jit(solution)/shard_map/backward_1/pallas_call | solution.py:324
  162.0 7.4 %backward_2.1 = bf16[6,360,512]{2,1,0:T(8,128)(2,1)} custom-call(s32[6]{0:T(128)S(1)} %compare_select_fusion.slot_ref, f32[6,8,512]{2,1,0:T(8,128)S(1)} %pad.30.base_ref, bf16[8,416,512]{2,1,0:T(8,128)(2,1)} %maximum_maximum_fusion.1.s0.s1.s2, bf16[8,416,512]{2,1,0:T(8,128)(2,1)} %maximum_maximum_fusion.1.s0.s1.s2, ...), custom_call_target="tpu_custom_call", output_to_operand_aliasing={{}: (8, {})} | custom-call | flops 2415919104 | bytes 7864320 | tf_op jit(solution)/shard_map/backward_2/pallas_call | solution.py:324
  (132 shorter events, 18.1 us)
Async XLA Ops:
  7.2 11.8 %copy-start.10 = (s32[6]{0:T(128)S(1)}, s32[6]{0:T(128)}, u32[]{:S(2)}) copy-start(s32[6]{0:T(128)} %constant.364) | copy-start | bytes 76
  7.2 12.4 %copy-start.13 = (s32[6]{0:T(128)S(1)}, s32[6]{0:T(128)}, u32[]{:S(2)}) copy-start(s32[6]{0:T(128)} %constant.381) | copy-start | bytes 76
  7.2 14.8 %copy-start.11 = (s32[6]{0:T(128)S(1)}, s32[6]{0:T(128)}, u32[]{:S(2)}) copy-start(s32[6]{0:T(128)} %constant.397) | copy-start | bytes 76
  7.2 18.3 %copy-start.9 = (s32[6]{0:T(128)S(1)}, s32[6]{0:T(128)}, u32[]{:S(2)}) copy-start(s32[6]{0:T(128)} %constant.413) | copy-start | bytes 76
  7.2 11.4 %copy-start.15 = (s32[48,3,8]{0,2,1:T(8,128)S(1)}, s32[48,3,8]{0,2,1:T(8,128)}, u32[]{:S(2)}) copy-start(s32[48,3,8]{0,2,1:T(8,128)} %param.31) | copy-start | bytes 13828
  7.2 11.5 %copy-start.14 = (f32[3,48,3,8]{1,3,2,0:T(8,128)S(1)}, f32[3,48,3,8]{1,3,2,0:T(8,128)}, u32[]{:S(2)}) copy-start(f32[3,48,3,8]{1,3,2,0:T(8,128)} %param.30) | copy-start | bytes 41476
  7.2 44.4 %all-gather.3.cloned.1.call-start = ((), (), s32[]{:S(2)}) async-start(), calls=%async_computation | async-start | bytes 3686400 | tf_op jit(solution)/shard_map/all_gather | solution.py:247
  9.2 18.2 %copy-start.12 = (s32[6]{0:T(128)S(1)}, s32[6]{0:T(128)}, u32[]{:S(2)}) copy-start(s32[6]{0:T(128)} %constant.430) | copy-start | bytes 76
  9.2 26.2 %collective-permute-start = (bf16[1,360,512]{2,1,0:T(8,128)(2,1)}, bf16[1,360,512]{2,1,0:T(8,128)(2,1)}, u32[]{:S(2)}, u32[]{:S(2)}) collective-permute-start(bf16[1,360,512]{2,1,0:T(8,128)(2,1)} %get-tuple-element.21), channel_id=1, source_target_pairs={{0,4},{4,8},{8,12},{12,16},{16,20},{20,24},{24,28},{1,5},{5,9},{9,... | collective-permute-start | bytes 1105928 | tf_op jit(solution)/shard_map/ppermute | solution.py:26
  14.9 21.7 %collective-permute-start.1 = (bf16[1,360,512]{2,1,0:T(8,128)(2,1)S(1)}, bf16[1,360,512]{2,1,0:T(8,128)(2,1)S(1)}, u32[]{:S(2)}, u32[]{:S(2)}) collective-permute-start(bf16[1,360,512]{2,1,0:T(8,128)(2,1)S(1)} %get-tuple-element.20), channel_id=1, source_target_pairs={{4,0},{8,4},{12,8},{16,12},{20,16},{24,20},{28,24},{5,1},{9,5},{13... | collective-permute-start | bytes 1105928 | tf_op jit(solution)/shard_map/ppermute | solution.py:27
  18.5 17.9 %copy-start.6 = (bf16[6,360,512]{2,1,0:T(8,128)(2,1)S(1)}, bf16[6,360,512]{2,1,0:T(8,128)(2,1)}, u32[]{:S(2)}) copy-start(bf16[6,360,512]{2,1,0:T(8,128)(2,1)} %state_ref.1) | copy-start | bytes 6635524
  18.5 117.1 %all-gather.5.cloned.1.call-start = ((), (), s32[]{:S(2)}) async-start(), calls=%async_computation.1 | async-start | bytes 1843200 | tf_op jit(solution)/shard_map/all_gather | solution.py:305
  18.9 3.7 %copy-start.8 = (f32[3,8,3,8]{3,0,2,1:T(4,128)}, f32[3,8,3,8]{3,0,2,1:T(4,128)S(1)}, u32[]{:S(2)}) copy-start(f32[3,8,3,8]{3,0,2,1:T(4,128)S(1)} %pad_dynamic-slice_fusion.2) | copy-start | bytes 6916
  36.6 1.6 copy-start.7
  38.2 7.3 %collective-permute-start.3 = (bf16[8,16,512]{2,1,0:T(8,128)(2,1)S(1)}, bf16[8,16,512]{2,1,0:T(8,128)(2,1)S(1)}, u32[]{:S(2)}, u32[]{:S(2)}) collective-permute-start(bf16[8,16,512]{2,1,0:T(8,128)(2,1)S(1)} %get-tuple-element.16), channel_id=1, source_target_pairs={{1,0},{2,1},{3,2},{0,3},{5,4},{6,5},{7,6},{4,7},{9,8},{10,9},{11,1... | collective-permute-start | bytes 393224 | tf_op jit(solution)/shard_map/ppermute | solution.py:32
  39.0 8.4 %collective-permute-start.2 = (bf16[8,16,512]{2,1,0:T(8,128)(2,1)S(1)}, bf16[8,16,512]{2,1,0:T(8,128)(2,1)S(1)}, u32[]{:S(2)}, u32[]{:S(2)}) collective-permute-start(bf16[8,16,512]{2,1,0:T(8,128)(2,1)S(1)} %get-tuple-element.15), channel_id=1, source_target_pairs={{0,1},{1,2},{2,3},{3,0},{4,5},{5,6},{6,7},{7,4},{8,9},{9,10},{10,1... | collective-permute-start | bytes 393224 | tf_op jit(solution)/shard_map/ppermute | solution.py:31
  51.7 11.0 %copy-start.4 = (bf16[3,512,512]{2,1,0:T(8,128)(2,1)S(1)}, bf16[3,512,512]{2,1,0:T(8,128)(2,1)}, u32[]{:S(2)}) copy-start(bf16[3,512,512]{2,1,0:T(8,128)(2,1)} %param.32) | copy-start | bytes 4718596
  61.2 1.5 copy-start.3
  80.3 15.6 %copy-start.1 = (bf16[6,360,512]{2,1,0:T(8,128)(2,1)}, bf16[6,360,512]{2,1,0:T(8,128)(2,1)S(1)}, u32[]{:S(2)}) copy-start(bf16[6,360,512]{2,1,0:T(8,128)(2,1)S(1)} %get-tuple-element.8.slope_ref) | copy-start | bytes 6635524
  95.1 19.7 %collective-permute-start.4 = (f32[2,8,3,64,128]{4,3,2,1,0:T(8,128)}, f32[2,8,3,64,128]{4,3,2,1,0:T(8,128)}, u32[]{:S(2)}, u32[]{:S(2)}) collective-permute-start(f32[2,8,3,64,128]{4,3,2,1,0:T(8,128)} %dynamic-slice_bitcast_fusion), channel_id=1, source_target_pairs={{0,1},{1,0},{2,3},{3,2},{4,5},{5,4},{6,7},{7,6},{8,9},{9,8},{10,11... | collective-permute-start | bytes 4718600 | tf_op jit(solution)/shard_map/ppermute | solution.py:56
  96.8 18.0 %collective-permute-start.9 = (bf16[1,360,512]{2,1,0:T(8,128)(2,1)S(1)}, bf16[1,360,512]{2,1,0:T(8,128)(2,1)S(1)}, u32[]{:S(2)}, u32[]{:S(2)}) collective-permute-start(bf16[1,360,512]{2,1,0:T(8,128)(2,1)S(1)} %get-tuple-element.19), channel_id=1, source_target_pairs={{0,4},{4,8},{8,12},{12,16},{16,20},{20,24},{24,28},{1,5},{5,9},{9,... | collective-permute-start | bytes 1105928 | tf_op jit(solution)/shard_map/ppermute | solution.py:26
  100.4 17.7 %copy-start.2 = (bf16[6,360,512]{2,1,0:T(8,128)(2,1)S(1)}, bf16[6,360,512]{2,1,0:T(8,128)(2,1)}, u32[]{:S(2)}) copy-start(bf16[6,360,512]{2,1,0:T(8,128)(2,1)} %copy-done.1) | copy-start | bytes 6635524
  100.4 17.9 %collective-permute-start.10 = (bf16[1,360,512]{2,1,0:T(8,128)(2,1)S(1)}, bf16[1,360,512]{2,1,0:T(8,128)(2,1)S(1)}, u32[]{:S(2)}, u32[]{:S(2)}) collective-permute-start(bf16[1,360,512]{2,1,0:T(8,128)(2,1)S(1)} %get-tuple-element.18), channel_id=1, source_target_pairs={{4,0},{8,4},{12,8},{16,12},{20,16},{24,20},{28,24},{5,1},{9,5},{13... | collective-permute-start | bytes 1105928 | tf_op jit(solution)/shard_map/ppermute | solution.py:27
  117.0 12.1 %collective-permute-start.5 = (bf16[1,8,3,64,128]{4,3,2,1,0:T(8,128)(2,1)S(1)}, bf16[1,8,3,64,128]{4,3,2,1,0:T(8,128)(2,1)S(1)}, u32[]{:S(2)}, u32[]{:S(2)}) collective-permute-start(bf16[1,8,3,64,128]{4,3,2,1,0:T(8,128)(2,1)S(1)} %dynamic-slice_convert_fusion), channel_id=1, source_target_pairs={{0,2},{1,3},{2,0},{3,1},{4,6},{5,7},{6,4},{7,5},{8,10},{9,11},{10,... | collective-permute-start | bytes 1179656 | tf_op jit(solution)/shard_map/ppermute | solution.py:56
  118.3 13.5 %collective-permute-start.12 = (bf16[8,16,512]{2,1,0:T(8,128)(2,1)S(1)}, bf16[8,16,512]{2,1,0:T(8,128)(2,1)S(1)}, u32[]{:S(2)}, u32[]{:S(2)}) collective-permute-start(bf16[8,16,512]{2,1,0:T(8,128)(2,1)S(1)} %get-tuple-element.14), channel_id=1, source_target_pairs={{1,0},{2,1},{3,2},{0,3},{5,4},{6,5},{7,6},{4,7},{9,8},{10,9},{11,1... | collective-permute-start | bytes 393224 | tf_op jit(solution)/shard_map/ppermute | solution.py:32
  118.7 13.1 %collective-permute-start.11 = (bf16[8,16,512]{2,1,0:T(8,128)(2,1)S(1)}, bf16[8,16,512]{2,1,0:T(8,128)(2,1)S(1)}, u32[]{:S(2)}, u32[]{:S(2)}) collective-permute-start(bf16[8,16,512]{2,1,0:T(8,128)(2,1)S(1)} %get-tuple-element.13), channel_id=1, source_target_pairs={{0,1},{1,2},{2,3},{3,0},{4,5},{5,6},{6,7},{7,4},{8,9},{9,10},{10,1... | collective-permute-start | bytes 393224 | tf_op jit(solution)/shard_map/ppermute | solution.py:31
  129.3 6.2 %collective-permute-start.6 = (bf16[4,3,64,128]{3,2,1,0:T(8,128)(2,1)S(1)}, bf16[4,3,64,128]{3,2,1,0:T(8,128)(2,1)S(1)}, u32[]{:S(2)}, u32[]{:S(2)}) collective-permute-start(bf16[4,3,64,128]{3,2,1,0:T(8,128)(2,1)S(1)} %fusion), channel_id=1, source_target_pairs={{0,4},{4,0},{8,12},{12,8},{16,20},{20,16},{24,28},{28,24},{1,5},{5... | collective-permute-start | bytes 589832 | tf_op jit(solution)/shard_map/ppermute | solution.py:56
  135.5 26.4 %collective-permute-start.7 = (f32[2,3,64,128]{3,2,1,0:T(8,128)S(1)}, f32[2,3,64,128]{3,2,1,0:T(8,128)S(1)}, u32[]{:S(2)}, u32[]{:S(2)}) collective-permute-start(f32[2,3,64,128]{3,2,1,0:T(8,128)S(1)} %dynamic-slice_bitcast_fusion.1), channel_id=1, source_target_pairs={{0,8},{4,12},{8,0},{12,4},{16,24},{20,28},{24,16},{28,20},{1,9},{5... | collective-permute-start | bytes 589832 | tf_op jit(solution)/shard_map/ppermute | solution.py:56
  135.6 1.4 copy-start.5
  137.0 9.8 %copy-start = (bf16[6,360,512]{2,1,0:T(8,128)(2,1)S(1)}, bf16[6,360,512]{2,1,0:T(8,128)(2,1)}, u32[]{:S(2)}) copy-start(bf16[6,360,512]{2,1,0:T(8,128)(2,1)} %cot_ref.7) | copy-start | bytes 6635524
  162.0 7.4 %collective-permute-start.8 = (f32[1,3,64,128]{3,2,1,0:T(8,128)S(1)}, f32[1,3,64,128]{3,2,1,0:T(8,128)S(1)}, u32[]{:S(2)}, u32[]{:S(2)}) collective-permute-start(f32[1,3,64,128]{3,2,1,0:T(8,128)S(1)} %constant_dynamic-slice_fusion), channel_id=1, source_target_pairs={{0,16},{4,20},{8,24},{12,28},{16,0},{20,4},{24,8},{28,12},{1,17},{... | collective-permute-start | bytes 294920 | tf_op jit(solution)/shard_map/ppermute | solution.py:56
Sparse Core Ops, SparseCore 0:
  18.6 31.8 all-gather.2
  98.5 21.2 all-gather.4
